TPU v7x, 256 devices: a whole 4x4x8 slice. The times are simulated.
256 devices in a mesh: ctx: 128 (over y, z, x_lo, core), head: 2 (over x_hi).
Axes of the slice: x: 4 (x_hi: 2, x_lo: 2; x = x_hi * 2 + x_lo), y: 4, z: 8, core: 2. Of those that a mesh axis runs over, the one named last changes fastest.
Arguments:
- hidden_in: bfloat16 [16384, 4096], P('ctx'), may hold values from -24 to 24
- queries: bfloat16 [16384, 2048], P('ctx', 'head'), may hold values from -32 to 32
- key_weight: bfloat16 [4096, 512], P('ctx', 'head'), may hold values from -0.09375 to 0.09375
- value_weight: bfloat16 [4096, 512], P('ctx', 'head'), may hold values from -0.09375 to 0.09375
- seg_ids: int32 [16384], replicated, may hold values from 0 to 31, never falling along the last dimension, each value on 1 to 4096 neighbouring positions
- grad_out: bfloat16 [16384, 2048], P('ctx', 'head'), may hold values from -6 to 6
Outputs:
- attended: bfloat16 [16384, 2048], P('ctx', 'head')
- grad_queries: bfloat16 [16384, 2048], P('ctx', 'head')
- grad_hidden: bfloat16 [16384, 4096], P('ctx')
- grad_key_weight: float32 [4096, 512], P('ctx', 'head')
- grad_value_weight: float32 [4096, 512], P('ctx', 'head')
All inputs are finite; a program needn't handle non-finite values.
Results may differ from a plain program's by a relative error of at most 0.029.
Values may be sent and summed in bfloat16 or wider, within the bound.
A program may use at most 64 MiB of HBM per device.

v0:
```python
import math

import jax
import jax.numpy as jnp
from jax import lax
from jax.sharding import PartitionSpec as P

HD = 128
WINDOW = 2048


NEG = -1e30


def shifted(x, axis, by):
    devices = lax.axis_size(axis)
    pairs = [(i, i + by) for i in range(devices) if 0 <= i + by < devices]
    return lax.ppermute(x, axis, pairs)


def shifted_2(x, axis, by):
    devices = lax.axis_size(axis)
    return lax.ppermute(x, axis, [(i, (i + by) % devices) for i in range(devices)])


def rotary_tables(positions, head_width):
    halfway = head_width // 2
    frequency = 10000.0 ** (-(jnp.arange(halfway, dtype=jnp.float32) * 2.0 / head_width))
    angles = positions.astype(jnp.float32)[:, None] * frequency[None, :]
    return (jnp.cos(angles)[:, None, :], jnp.sin(angles)[:, None, :])


def rotate(vectors, cosine, sine_table):
    halfway = vectors.shape[-1] // 2
    lower_half = vectors[..., :halfway]
    upper_half = vectors[..., halfway:]
    return jnp.concatenate(
        [
            lower_half * cosine - upper_half * sine_table,
            upper_half * cosine + lower_half * sine_table,
        ],
        axis=-1,
    )


def unrotate(gradient, cosine, sine_table):
    halfway = gradient.shape[-1] // 2
    lower_half = gradient[..., :halfway]
    upper_half = gradient[..., halfway:]
    return jnp.concatenate(
        [
            lower_half * cosine + upper_half * sine_table,
            upper_half * cosine - lower_half * sine_table,
        ],
        axis=-1,
    )


def body(hidden_in, queries, key_weight, value_weight, seg_ids, grad_out):
    row_count = hidden_in.shape[0]
    kv_cols = key_weight.shape[1]
    kv_heads = kv_cols // HD
    group = queries.shape[1] // kv_cols
    loop_size = lax.axis_size("ctx")
    own_index = lax.axis_index("ctx")
    hop_count = min(WINDOW // row_count, loop_size - 1)
    scaling = 1.0 / math.sqrt(HD)
    weight_pair = jnp.concatenate([key_weight, value_weight], axis=1)
    full_weights = lax.all_gather(weight_pair, "ctx", axis=0, tiled=True)
    projected = jnp.dot(hidden_in, full_weights, preferred_element_type=jnp.float32)
    offsets = jnp.arange(row_count, dtype=jnp.int32)
    positions = own_index * row_count + offsets
    cosine, sine_table = rotary_tables(positions, HD)
    key_rows = rotate(
        projected[:, :kv_cols].reshape(row_count, kv_heads, HD), cosine, sine_table
    ).astype(jnp.bfloat16)
    value_rows = projected[:, kv_cols:].reshape(row_count, kv_heads, HD).astype(jnp.bfloat16)
    own_pair = jnp.stack([key_rows, value_rows])
    query_heads = queries.reshape(row_count, kv_heads, group, HD)
    out_grads = grad_out.reshape(row_count, kv_heads, group, HD)
    query_seg = lax.dynamic_slice_in_dim(seg_ids, own_index * row_count, row_count)

    def allowed_for(distance):
        block_index = (own_index - distance) % loop_size
        key_pos = block_index * row_count + offsets
        key_seg = lax.dynamic_slice_in_dim(seg_ids, block_index * row_count, row_count)
        spacing = positions[:, None] - key_pos[None, :]
        return (query_seg[:, None] == key_seg[None, :]) & (spacing >= 0) & (spacing < WINDOW)

    def scores_of(key_block, allowed):
        scores = (
            jnp.einsum("qkgd,lkd->kgql", query_heads, key_block, preferred_element_type=jnp.float32)
            * scaling
        )
        return jnp.where(allowed[None, None], scores, NEG)

    def forward_update(state, pair, allowed):
        best, total, accum = state
        scores = scores_of(pair[0], allowed)
        new_best = jnp.maximum(best, jnp.max(scores, axis=-1))
        retain = jnp.exp(best - new_best)
        expo = jnp.where(allowed[None, None], jnp.exp(scores - new_best[..., None]), 0.0)
        total = total * retain + jnp.sum(expo, axis=-1)
        accum = accum * retain[..., None] + jnp.einsum(
            "kgql,lkd->kgqd", expo.astype(jnp.bfloat16), pair[1], preferred_element_type=jnp.float32
        )
        return (new_best, total, accum)

    def forward_step(state, distance, pair):
        allowed = allowed_for(distance)
        return forward_update(state, pair, allowed)

    start_state = (
        jnp.full((kv_heads, group, row_count), NEG, jnp.float32),
        jnp.zeros((kv_heads, group, row_count), jnp.float32),
        jnp.zeros((kv_heads, group, row_count, HD), jnp.float32),
    )
    state = forward_step(start_state, 0, own_pair)

    def forward_turn(carry, distance):
        inner, pair = carry
        pair = shifted(pair, "ctx", 1)
        inner = forward_step(inner, distance, pair)
        return ((inner, pair), pair)

    distances = jnp.arange(1, hop_count + 1, dtype=jnp.int32)
    (state, last_pair), stored = lax.scan(forward_turn, (state, own_pair), distances, unroll=2)
    best, total, accum = state
    mixed_low = (accum / total[..., None]).astype(jnp.bfloat16)
    attended = mixed_low.transpose(2, 0, 1, 3).reshape(row_count, kv_heads * group * HD)
    log_total = best + jnp.log(total)
    delta = jnp.sum(
        out_grads.astype(jnp.float32).transpose(1, 2, 0, 3) * mixed_low.astype(jnp.float32), axis=-1
    )

    def grad_parts(pair, allowed):
        scores = scores_of(pair[0], allowed)
        probs = jnp.where(allowed[None, None], jnp.exp(scores - log_total[..., None]), 0.0)
        dprobs = jnp.einsum(
            "qkgd,lkd->kgql", out_grads, pair[1], preferred_element_type=jnp.float32
        )
        dscores = probs * (dprobs - delta[..., None])
        probs_low = probs.astype(jnp.bfloat16)
        dscores_low = dscores.astype(jnp.bfloat16)
        query_part = jnp.einsum(
            "kgql,lkd->kgqd", dscores_low, pair[0], preferred_element_type=jnp.float32
        )
        key_part = (
            jnp.einsum(
                "kgql,qkgd->lkd", dscores_low, query_heads, preferred_element_type=jnp.float32
            )
            * scaling
        )
        value_part = jnp.einsum(
            "kgql,qkgd->lkd", probs_low, out_grads, preferred_element_type=jnp.float32
        )
        return (query_part, jnp.stack([key_part, value_part]))

    def backward_step(distance, pair):
        allowed = allowed_for(distance)
        return grad_parts(pair, allowed)

    query_acc, chain = backward_step(0, own_pair)

    def outward_turn(carry, packed):
        query_sum, moving = carry
        distance, pair = packed
        moving = shifted_2(moving, "ctx", 1)
        query_part, pair_part = backward_step(distance, pair)
        return ((query_sum + query_part, moving + pair_part), None)

    (query_acc, chain), _ = lax.scan(
        outward_turn, (query_acc, chain), (distances, stored), unroll=2
    )
    chain = shifted_2(chain, "ctx", -hop_count)
    grad_queries = (
        (query_acc * scaling)
        .astype(jnp.bfloat16)
        .transpose(2, 0, 1, 3)
        .reshape(row_count, kv_heads * group * HD)
    )
    key_grad = (
        unrotate(chain[0], cosine, sine_table).reshape(row_count, kv_cols).astype(jnp.bfloat16)
    )
    value_grad = chain[1].reshape(row_count, kv_cols).astype(jnp.bfloat16)
    grad_pair = jnp.concatenate([key_grad, value_grad], axis=1)
    partial_hidden = jnp.einsum(
        "tc,dc->td", grad_pair, full_weights, preferred_element_type=jnp.float32
    )
    grad_hidden = lax.psum(partial_hidden, "head").astype(jnp.bfloat16)
    weight_grads = lax.psum_scatter(
        jnp.einsum("tr,tc->rc", hidden_in, grad_pair, preferred_element_type=jnp.float32),
        "ctx",
        scatter_dimension=0,
        tiled=True,
    )
    return (
        attended,
        grad_queries,
        grad_hidden,
        weight_grads[:, :kv_cols],
        weight_grads[:, kv_cols:],
    )


def solution(mesh):
    placed = (
        P("ctx", None),
        P("ctx", "head"),
        P("ctx", "head"),
        P("ctx", "head"),
        P(),
        P("ctx", "head"),
    )
    return jax.shard_map(
        body,
        mesh=mesh,
        in_specs=placed,
        out_specs=(
            P("ctx", "head"),
            P("ctx", "head"),
            P("ctx", None),
            P("ctx", "head"),
            P("ctx", "head"),
        ),
        check_vma=False,
    )
```

profile of v0, /device:TPU:1, one launch (start us, length us, event | category | flops | bytes accessed | tf_op | source)
XLA Modules:
  0.0 1179.4 jit_solution(16243524007381576825)
XLA Ops:
  12.7 216.9 %all-gather.2.cloned.1.call-done = bf16[4096,512]{1,0:T(8,128)(2,1)} async-done(((bf16[32,512]{1,0:T(8,128)(2,1)}), bf16[4096,512]{1,0:T(8,128)(2,1)}) %all-gather.2.cloned.1.call-update) | async-done | bytes 4194320 | tf_op jit(solution)/shard_map/all_gather | solution.py:69
  229.6 3.5 convolution_bitcast_fusion.8
  235.1 127.9 %while.38 = (s32[]{:T(128)}, f32[2,4,128]{2,1,0:T(4,128)S(1)}, f32[2,4,128]{2,1,0:T(4,128)S(1)}, f32[2,4,128,128]{3,2,1,0:T(8,128)S(1)}, bf16[2,128,2,128]{3,1,2...) while((s32[]{:T(128)}, f32[2,4,128]{2,1,0:T(4,128)S(1)}, ...), condition=%wide.region_7.8_spmd.clone.clone, body=%wide.region_2.7_spmd.clone.clone.sunk | while | flops 137826720 | bytes 7847039 | solution.py:127
  235.1 4.0 collective-permute-start
  249.3 4.4 collective-permute-start
  257.8 3.1 collective-permute-start.1
  264.7 4.4 collective-permute-start
  273.2 3.9 collective-permute-start.1
  281.1 4.4 collective-permute-start
  289.6 4.0 collective-permute-start.1
  297.5 4.3 collective-permute-start
  305.9 4.0 collective-permute-start.1
  313.9 4.4 collective-permute-start
  322.3 4.0 collective-permute-start.1
  330.2 4.3 collective-permute-start
  338.7 4.0 collective-permute-start.1
  346.6 4.4 collective-permute-start
  355.1 4.0 collective-permute-start.1
  369.7 176.0 %while.39 = (s32[]{:T(128)}, f32[2,4,128,128]{3,2,1,0:T(8,128)S(1)}, f32[2,128,2,128]{3,1,2,0:T(8,128)}, s32[128]{0:T(128)S(1)}, s32[8,2]{0,1:T(2,128)S(1)}, /*i...) while((s32[]{:T(128)}, ...), condition=%wide.region_10.11_spmd.clone.clone, body=%wide.region_9.10_spmd.clone.clone.sunk | while | flops 338428320 | bytes 13589695 | solution.py:172
  423.1 4.9 collective-permute-done.3
  442.4 8.8 collective-permute-done.3
  465.6 8.8 collective-permute-done.3
  488.8 8.8 collective-permute-done.3
  512.0 8.8 collective-permute-done.3
  535.2 8.8 collective-permute-done.3
  545.7 4.4 collective-permute-start.4
  550.0 5.4 collective-permute-done.4
  555.9 4.5 convolution_bitcast_fusion.6
  560.4 9.0 copy.111
  572.4 5.1 fusion.84
  577.5 47.0 %all-reduce.1 = bf16[128,4096]{1,0:T(8,128)(2,1)} all-reduce(f32[128,4096]{1,0:T(8,128)} %fusion.84), channel_id=1, replica_groups=mesh['ctx'=128,'head'=2] {'head'}, use_global_device_ids=true, to_apply=%region_11.12 | all-reduce | flops 524288 | bytes 3145728 | tf_op jit(solution)/shard_map/psum | solution.py:190
  624.5 546.6 %reduce-scatter.4.cloned.1.call-done = f32[32,512]{1,0:T(8,128)} async-done(((f32[4096,512]{1,0:T(8,128)}), f32[32,512]{1,0:T(8,128)}) %reduce-scatter.4.cloned.1.call-update) | async-done | bytes 65552
  (370 shorter events, 189.6 us)
Async XLA Ops:
  7.2 222.4 %all-gather.2.cloned.1.call-start = ((), (), s32[]{:S(2)}) async-start(), calls=%async_computation.1 | async-start | bytes 4227072 | tf_op jit(solution)/shard_map/all_gather | solution.py:69
  8.7 1162.5 %reduce-scatter.4.cloned.1.call-start = ((), (), s32[]{:S(2)}) async-start(), calls=%async_computation.2 | async-start | bytes 8454144
  235.1 8.0 collective-permute-start
  249.3 8.5 collective-permute-start
  264.7 8.5 collective-permute-start
  273.2 5.9 collective-permute-start.1
  281.1 8.5 collective-permute-start
  289.6 5.9 collective-permute-start.1
  297.5 8.4 collective-permute-start
  305.9 6.0 collective-permute-start.1
  313.9 8.5 collective-permute-start
  322.3 5.9 collective-permute-start.1
  330.2 8.5 collective-permute-start
  338.7 5.9 collective-permute-start.1
  346.6 8.5 collective-permute-start
  355.1 5.9 collective-permute-start.1
  369.7 11.6 collective-permute-start.2
  382.2 5.5 collective-permute-start.3
  389.4 11.8 collective-permute-start.2
  408.0 11.8 collective-permute-start.2
  420.8 7.2 collective-permute-start.3
  429.7 10.3 collective-permute-start.2
  441.0 10.2 collective-permute-start.3
  452.9 10.3 collective-permute-start.2
  464.2 10.2 collective-permute-start.3
  476.1 10.3 collective-permute-start.2
  487.4 10.2 collective-permute-start.3
  499.3 10.3 collective-permute-start.2
  510.6 10.2 collective-permute-start.3
  522.5 10.3 collective-permute-start.2
  533.8 10.2 collective-permute-start.3
  545.7 9.7 collective-permute-start.4
  (14 other events, 1284.8 us)
Sparse Core Ops, SparseCore 0:
  10.5 219.1 all-gather.1
  569.6 601.5 reduce-scatter.3
where the time goes:
time: 1190 us; the launch traced here: 1180 us
  waiting for transfers between devices  841 us (71%)
  matrix products  86.1 us (7%)
  starting transfers between devices  80 us (7%)
  other arithmetic  59.5 us (5%)
  blocking collectives  47 us (4%)
  local copies, waits for them, and re-layouts  28.6 us (2%)
  loops' own time  23 us (2%)
  between operations  14.4 us (1%)
    unnamed x3, waiting for transfers between devices  547 us
    all_gather x1, waiting for transfers between devices, body(): full_weights = lax.all_gather(weight_pair, 'ctx', axis=0, tiled=True)  217 us
    ppermute x17, waiting for transfers between devices, shifted_2(): lax.ppermute(x, axis, [(i, (i + by) % devices) for i in range(devices)])  63.8 us
    ppermute x16, starting transfers between devices, shifted(): return lax.ppermute(x, axis, pairs)  63.5 us
    psum x1, blocking collectives, body(): grad_hidden = lax.psum(partial_hidden, 'head').astype(jnp.bfloat16)  47 us
  transfers between devices with their start and end apart: 35, of which 24 were waited for; matrix products, arithmetic and copies ran while one was open for 9% of the time, Pallas kernels for 0%

commit v1 on v0

v1 whole, which is shorter than its diff:
```python
import functools
import math

import jax
import jax.numpy as jnp
from jax import lax
from jax.experimental import pallas as pl
from jax.experimental.pallas import tpu as pltpu
from jax.sharding import PartitionSpec as P

HD = 128
WINDOW = 2048
NEG = -1e30
MESH = pl.DeviceIdType.MESH
VM = pl.BlockSpec(memory_space=pltpu.VMEM)
ANY = pl.BlockSpec(memory_space=pl.ANY)
BF = jnp.bfloat16
F32 = jnp.float32
NY, NZ = 4, 8
DZ = (1, -1, 2, -2, 3, -3, 4)
DY = (1, -1, 2)


def coords():
    i = lax.axis_index("ctx")
    h = lax.axis_index("head")
    return i // 32, (i // 4) % 8, (i // 2) % 2, i % 2, h


def dev(y, z, x, c, h):
    return (((y % NY) * NZ + z % NZ) * 4 + x * 2 + c, h)


def plane_dev(p, x, c, h):
    return ((p % 32) * 4 + x * 2 + c, h)


def enter(partners):
    barrier = pltpu.get_barrier_semaphore()
    for partner in partners:
        pl.semaphore_signal(barrier, inc=1, device_id=partner, device_id_type=MESH)
    pl.semaphore_wait(barrier, len(partners))


def push(src, dst, send, recv, to):
    copy = pltpu.make_async_remote_copy(
        src_ref=src, dst_ref=dst, send_sem=send, recv_sem=recv, device_id=to, device_id_type=MESH
    )
    copy.start()
    return copy


def arrived(dst, send, recv, to):
    pltpu.make_async_remote_copy(
        src_ref=dst, dst_ref=dst, send_sem=send, recv_sem=recv, device_id=to, device_id_type=MESH
    ).wait_recv()


def params(cid):
    return pltpu.CompilerParams(
        collective_id=cid, has_side_effects=True, vmem_limit_bytes=56 * 2**20
    )


def gather_kernel(
    wk, wv, hid, q, do, w, hid2, q2, do2, loc, core_s, core_r, x_s, x_r, send, recv
):
    y, z, x, c, h = coords()
    other = dev(y, z, x, 1 - c, h)
    mate = dev(y, z, 1 - x, c, h)
    ys = [dev(y + d, z, x, c, h) for d in DY]
    zs = [dev(y, z + d, x, c, h) for d in DZ]
    enter([other, mate] + ys + zs)
    rows = pl.ds(c * 32, 32)
    theirs = pl.ds(pl.multiple_of((1 - c) * HD, HD), HD)
    mine = pl.ds(pl.multiple_of(c * HD, HD), HD)
    theirs_q = pl.ds(pl.multiple_of((1 - c) * 512, 512), 512)
    mine_q = pl.ds(pl.multiple_of(c * 512, 512), 512)
    toks = pl.ds(pl.multiple_of(c * 128, 128), 128)
    moves = [
        (wk.at[:, theirs], wk.at[:, mine], w.at[y, z, x, rows, pl.ds(0, HD)]),
        (wv.at[:, theirs], wv.at[:, mine], w.at[y, z, x, rows, pl.ds(HD, HD)]),
        (q.at[:, theirs_q], q.at[:, mine_q], q2.at[toks]),
        (do.at[:, theirs_q], do.at[:, mine_q], do2.at[toks]),
        (hid, hid, hid2.at[toks]),
    ]
    crossing, local = [], []
    for n, (out, own, dst) in enumerate(moves):
        crossing.append(push(out, dst, core_s.at[n], core_r.at[n], other))
        copy = pltpu.make_async_copy(own, dst, loc.at[n])
        copy.start()
        local.append(copy)
    for n in range(2):
        crossing[n].wait_recv()
        local[n].wait()
    pair = push(w.at[y, z, x], w.at[y, z, x], x_s, x_r, mate)
    pair.wait_recv()

    def slot(yy, zz):
        return recv.at[(yy % NY) * NZ + zz % NZ]

    def wait_plane(yy, zz):
        arrived(w.at[yy % NY, zz % NZ], send.at[0], slot(yy, zz), other)

    @pl.when(c == 0)
    def _():
        sent = []

        def go(yy, zz, to):
            ref = w.at[yy % NY, zz % NZ]
            sent.append(push(ref, ref, send.at[len(sent)], slot(yy, zz), to))

        for to in zs:
            go(y, z, to)
        for to in ys:
            go(y, z, to)
        for d in DZ:
            wait_plane(y, z + d)
            for to in ys:
                go(y, z + d, to)
        for d in (0,) + DZ:
            for e in DY:
                wait_plane(y + e, z + d)
        for copy in sent:
            copy.wait_send()

    @pl.when(c == 1)
    def _():
        sent = []

        def go(yy, zz, to):
            ref = w.at[yy % NY, zz % NZ]
            sent.append(push(ref, ref, send.at[len(sent)], slot(yy, zz), to))

        for to in ys:
            go(y, z, to)
        up, down = zs[0], zs[1]
        for s in range(4):
            for n, e in enumerate((0,) + DY):
                if s == 0:
                    if e:
                        wait_plane(y + e, z)
                    go(y + e, z, up)
                    go(y + e, z, down)
                    continue
                wait_plane(y + e, z - s)
                if s < 3 or n < 2:
                    go(y + e, z - s, up)
                wait_plane(y + e, z + s)
                if s < 3 or n >= 2:
                    go(y + e, z + s, down)
        for e in (0,) + DY:
            wait_plane(y + e, z + 4)
        for copy in sent:
            copy.wait_send()

    pair.wait_send()
    for n in range(5):
        crossing[n].wait_send()
        if n >= 2:
            crossing[n].wait_recv()
            local[n].wait()


def gather_weights(wk, wv, hid, q, do):
    dma = pltpu.SemaphoreType.DMA
    return pl.pallas_call(
        gather_kernel,
        out_shape=(
            jax.ShapeDtypeStruct((NY, NZ, 2, 64, 256), BF),
            jax.ShapeDtypeStruct((256, 4096), BF),
            jax.ShapeDtypeStruct((256, 512), BF),
            jax.ShapeDtypeStruct((256, 512), BF),
        ),
        in_specs=[VM, VM, ANY, ANY, ANY],
        out_specs=(VM, ANY, ANY, ANY),
        scratch_shapes=[dma((5,)), dma((5,)), dma((5,)), dma, dma, dma((31,)), dma((32,))],
        compiler_params=params(0),
        name="gather",
    )(wk, wv, hid, q, do)


def window_kernel(kv, w, win, wo, loc, core_s, core_r, z_s, z_r, x_s, x_r):
    y, z, x, c, h = coords()
    p = y * NZ + z
    other = dev(y, z, x, 1 - c, h)
    mate = dev(y, z, 1 - x, c, h)
    near = [plane_dev(p + d, x, c, h) for d in (1, -1, 2, -2, 4, -4)]
    enter([other, mate] + near)
    up1, up2, up4 = near[0], near[2], near[4]
    sent = [
        push(kv, win.at[3, x], z_s.at[0], z_r.at[3], up1),
        push(kv, win.at[2, x], z_s.at[1], z_r.at[2], up2),
        push(kv, win.at[0, x], z_s.at[2], z_r.at[0], up4),
    ]
    own = pltpu.make_async_copy(kv, win.at[4, x], loc)
    own.start()

    def across(k, src):
        j = 4 - x - k
        return push(src, win.at[k, x], x_s.at[j], x_r.at[j], mate)

    @pl.when(x == 0)
    def _():
        across(4, kv)

    weights = push(w, wo, core_s, core_r, other)

    def got(k):
        arrived(win.at[k, x], z_s.at[0], z_r.at[k], up1)

    got(3)
    across(3, win.at[3, x])
    got(2)
    sent.append(push(win.at[2, x], win.at[1, x], z_s.at[3], z_r.at[1], up1))
    across(2, win.at[2, x])
    got(0)

    @pl.when(x == 1)
    def _():
        across(0, win.at[0, x])

    got(1)
    across(1, win.at[1, x])
    for j in range(4):
        arrived(win.at[3 + x - j, 1 - x], x_s.at[j], x_r.at[j], mate)
    for copy in sent:
        copy.wait_send()
    for j in range(4):
        pltpu.make_async_remote_copy(
            src_ref=kv, dst_ref=win.at[4 - x - j, x], send_sem=x_s.at[j], recv_sem=x_r.at[j],
            device_id=mate, device_id_type=MESH,
        ).wait_send()
    own.wait()
    weights.wait()


def exchange_window(kv, w):
    dma = pltpu.SemaphoreType.DMA
    return pl.pallas_call(
        window_kernel,
        out_shape=(
            jax.ShapeDtypeStruct((5, 2, 256, 256), BF),
            jax.ShapeDtypeStruct(w.shape, BF),
        ),
        in_specs=[VM, ANY],
        out_specs=(VM, ANY),
        scratch_shapes=[dma, dma, dma, dma((4,)), dma((4,)), dma((4,)), dma((4,))],
        compiler_params=params(1),
        name="window",
    )(kv, w)


def attention_kernel(q2, do2, win, seg, att, gq, dkv, s_ref, acc):
    i = lax.axis_index("ctx")
    x = (i // 2) % 2
    chip = i // 2
    base = x * 256
    scaling = 1.0 / math.sqrt(HD)
    to2 = scaling * math.log2(math.e)
    acc[...] = jnp.zeros_like(acc)
    key_row = lax.broadcasted_iota(jnp.int32, (128, 128), 0)
    query_col = lax.broadcasted_iota(jnp.int32, (128, 128), 1)
    tilt = query_col - key_row
    nt = (((0,), (0,)), ((), ()))

    def dot(a, b):
        return jnp.dot(a, b, preferred_element_type=F32)

    for t in range(2):
        block = chip * 2 + t
        rows = pl.ds(t * 128, 128)
        q = jnp.concatenate([q2[rows, g * HD : (g + 1) * HD] for g in range(4)], axis=0)
        do = jnp.concatenate([do2[rows, g * HD : (g + 1) * HD] for g in range(4)], axis=0)
        q_t = q.T
        do_t = do.T
        seg_q = seg[pl.ds(block, 1), :]

        def keys_at(b):
            return pl.ds(pl.multiple_of(base + (b + t) * 128, 128), 128)

        def score(b, best):
            k = win[keys_at(b), 0:HD]
            index = block - 16 + b
            seg_k = seg[pl.ds(jnp.maximum(index, 0), 1), :]
            seg_k = jnp.where(index >= 0, seg_k, -1.0)
            seg_k = jnp.broadcast_to(seg_k, (128, 128)).T
            gap = tilt + (16 - b) * 128
            ok = (seg_k == seg_q) & (gap >= 0) & (gap < WINDOW)
            bias = jnp.where(ok, 0.0, NEG)
            s = dot(k, q_t) * to2 + jnp.concatenate([bias] * 4, axis=1)
            s_ref[pl.ds(pl.multiple_of(b * 128, 128), 128), :] = s
            return jnp.maximum(best, jnp.max(s, axis=0, keepdims=True))

        best = lax.fori_loop(0, 17, score, jnp.full((1, 512), NEG, F32))

        def mix(b, carry):
            total, out = carry
            where = pl.ds(pl.multiple_of(b * 128, 128), 128)
            e = jnp.exp2(s_ref[where, :] - best)
            s_ref[where, :] = e
            v = win[keys_at(b), HD : 2 * HD]
            out = out + lax.dot_general(v, e.astype(BF), nt, preferred_element_type=F32)
            return total + jnp.sum(e, axis=0, keepdims=True), out

        total, out = lax.fori_loop(
            0, 17, mix, (jnp.zeros((1, 512), F32), jnp.zeros((HD, 512), F32))
        )
        inverse = 1.0 / total
        low = (out * inverse).astype(BF)
        delta = jnp.sum(low.astype(F32) * do_t.astype(F32), axis=0, keepdims=True)
        for g in range(4):
            att[rows, g * HD : (g + 1) * HD] = low[:, g * HD : (g + 1) * HD].T

        def back(b, query_sum):
            where = pl.ds(pl.multiple_of(b * 128, 128), 128)
            k = win[keys_at(b), 0:HD]
            v = win[keys_at(b), HD : 2 * HD]
            probs = s_ref[where, :] * inverse
            dscores = probs * (dot(v, do_t) - delta)
            probs = probs.astype(BF)
            dscores = dscores.astype(BF)
            into = pl.ds(pl.multiple_of((b + t) * 128, 128), 128)
            acc[into, 0:HD] += dot(dscores, q)
            acc[into, HD : 2 * HD] += dot(probs, do)
            return query_sum + lax.dot_general(k, dscores, nt, preferred_element_type=F32)

        query_sum = lax.fori_loop(0, 17, back, jnp.zeros((HD, 512), F32))
        query_low = (query_sum * scaling).astype(BF)
        for g in range(4):
            gq[rows, g * HD : (g + 1) * HD] = query_low[:, g * HD : (g + 1) * HD].T

    def finish(b, _):
        src = pl.ds(pl.multiple_of(b * 128, 128), 128)
        dst = pl.ds(pl.multiple_of(base + b * 128, 128), 128)
        dkv[dst, 0:HD] = (acc[src, 0:HD] * scaling).astype(BF)
        dkv[dst, HD : 2 * HD] = acc[src, HD : 2 * HD].astype(BF)
        return 0

    lax.fori_loop(0, 18, finish, 0)


def attention(q2, do2, win, seg):
    return pl.pallas_call(
        attention_kernel,
        out_shape=(
            jax.ShapeDtypeStruct((256, 512), BF),
            jax.ShapeDtypeStruct((256, 512), BF),
            jax.ShapeDtypeStruct((2560, 256), BF),
        ),
        in_specs=[VM] * 4,
        out_specs=(VM,) * 3,
        scratch_shapes=[pltpu.VMEM((2176, 512), F32), pltpu.VMEM((2304, 256), F32)],
        compiler_params=pltpu.CompilerParams(vmem_limit_bytes=56 * 2**20),
        name="attention",
    )(q2, do2, win, seg)


def return_kernel(
    dkv, att2, gq2, cos, sin, kvg, kvo, att, gq,
    own, x_in, z_in, core_s, core_r, x_s, x_r, z_s, z_r, loc
):
    y, z, x, c, h = coords()
    p = y * NZ + z
    other = dev(y, z, x, 1 - c, h)
    mate = dev(y, z, 1 - x, c, h)
    near = [plane_dev(p + d, x, c, h) for d in (-1, 1, -2, 2, -4, 4)]
    enter([other, mate] + near)
    down1, down2, down4 = near[0], near[2], near[4]
    theirs = pl.ds(pl.multiple_of((1 - c) * 128, 128), 128)
    mine = pl.ds(pl.multiple_of(c * 128, 128), 128)
    cols = pl.ds(pl.multiple_of(c * 512, 512), 512)
    crossing = []
    for j in (3, 2, 1, 0):
        crossing.append(
            push(dkv.at[3 + x - j, 1 - x], x_in.at[j], x_s.at[j], x_r.at[j], mate)
        )
    waits = []
    for n, (src, dst) in enumerate(((att2, att), (gq2, gq))):
        waits.append(push(src.at[theirs], dst.at[:, cols], core_s.at[n], core_r.at[n], other))
        copy = pltpu.make_async_copy(src.at[mine], dst.at[:, cols], loc.at[n])
        copy.start()
        waits.append(copy)

    def merge(k, with_mate):
        if with_mate is None:
            own[k] = dkv[k, x]
        else:
            own[k] = (dkv[k, x].astype(F32) + x_in[with_mate].astype(F32)).astype(BF)

    @pl.when(x == 0)
    def _():
        merge(0, None)

    @pl.when(x == 1)
    def _():
        arrived(x_in.at[3], x_s.at[3], x_r.at[3], mate)
        merge(0, 3)

    sent = [push(own.at[0], z_in.at[0], z_s.at[0], z_r.at[0], down4)]
    for k in (1, 2, 3):
        j = 4 - x - k
        arrived(x_in.at[j], x_s.at[j], x_r.at[j], mate)
        merge(k, j)
        if k == 1:
            sent.append(push(own.at[1], z_in.at[1], z_s.at[1], z_r.at[1], down1))
        if k == 3:
            sent.append(push(own.at[3], z_in.at[3], z_s.at[3], z_r.at[3], down1))
    arrived(z_in.at[1], z_s.at[1], z_r.at[1], down1)
    own[2] = (own[2].astype(F32) + z_in[1].astype(F32)).astype(BF)
    sent.append(push(own.at[2], z_in.at[2], z_s.at[2], z_r.at[2], down2))

    @pl.when(x == 0)
    def _():
        arrived(x_in.at[0], x_s.at[0], x_r.at[0], mate)
        merge(4, 0)

    @pl.when(x == 1)
    def _():
        merge(4, None)

    for k in (3, 0, 2):
        arrived(z_in.at[k], z_s.at[k], z_r.at[k], down1)
    total = (
        own[4].astype(F32) + z_in[3].astype(F32) + z_in[0].astype(F32) + z_in[2].astype(F32)
    )
    keys = total[:, 0:HD]
    keys = keys * cos[...] + pltpu.roll(keys, 64, 1) * sin[...]
    kvg[:, 0:HD] = keys.astype(BF)
    kvg[:, HD : 2 * HD] = total[:, HD : 2 * HD].astype(BF)
    waits.append(push(kvg.at[theirs], kvo, core_s.at[2], core_r.at[2], other))
    for copy in crossing:
        copy.wait_send()
    for copy in sent:
        copy.wait_send()
    for copy in waits:
        copy.wait()


def return_gradients(dkv, att2, gq2, cos, sin):
    dma = pltpu.SemaphoreType.DMA
    return pl.pallas_call(
        return_kernel,
        out_shape=(
            jax.ShapeDtypeStruct((256, 256), BF),
            jax.ShapeDtypeStruct((128, 256), BF),
            jax.ShapeDtypeStruct((128, 1024), BF),
            jax.ShapeDtypeStruct((128, 1024), BF),
        ),
        in_specs=[VM, VM, VM, VM, VM],
        out_specs=(VM, VM, VM, VM),
        scratch_shapes=[
            pltpu.VMEM((5, 256, 256), BF),
            pltpu.VMEM((4, 256, 256), BF),
            pltpu.VMEM((4, 256, 256), BF),
            dma((3,)),
            dma((3,)),
            dma((4,)),
            dma((4,)),
            dma((4,)),
            dma((4,)),
            dma((2,)),
        ],
        compiler_params=params(2),
        name="returns",
    )(dkv, att2, gq2, cos, sin)


def sums_kernel(
    ph, wg, gh, gk, gv, h_in, buf0, acc0, zin0, buf1, acc1, yin1, part, x_in, chunk, c_in,
    h_s, h_r, a_s, a_r, b_s, b_r, x_s, x_r, c_s, c_r
):
    y, z, x, c, h = coords()
    other = dev(y, z, x, 1 - c, h)
    mate = dev(y, z, 1 - x, c, h)
    peer = dev(y, z, x, c, 1 - h)
    ys = [dev(y + d, z, x, c, h) for d in DY]
    zs = [dev(y, z + d, x, c, h) for d in DZ]
    enter([other, mate, peer] + ys + zs)
    hidden = push(ph, h_in, h_s, h_r, peer)

    @pl.when(c == 0)
    def _():
        first = [
            push(wg.at[(y + d) % NY], buf0.at[n], a_s.at[n], a_r.at[n], ys[n])
            for n, d in enumerate(DY)
        ]
        for copy in first:
            copy.wait_recv()

        def add(zz, _):
            acc0[zz] = (
                wg[y, zz].astype(F32)
                + buf0[0, zz].astype(F32)
                + buf0[1, zz].astype(F32)
                + buf0[2, zz].astype(F32)
            ).astype(BF)
            return 0

        lax.fori_loop(0, NZ, add, 0)
        second = [
            push(acc0.at[(z + d) % NZ], zin0.at[n], b_s.at[n], b_r.at[n], zs[n])
            for n, d in enumerate(DZ)
        ]
        total = acc0[z].astype(F32)
        for n, copy in enumerate(second):
            copy.wait_recv()
            total = total + zin0[n].astype(F32)
        part[...] = total
        for copy in first + second:
            copy.wait_send()

    @pl.when(c == 1)
    def _():
        first = [
            push(wg.at[:, (z + d) % NZ], buf1.at[n], a_s.at[n], a_r.at[n], zs[n])
            for n, d in enumerate(DZ)
        ]
        for copy in first:
            copy.wait_recv()

        def add(yy, _):
            total = wg[yy, z].astype(F32)
            for n in range(7):
                total = total + buf1[n, yy].astype(F32)
            acc1[yy] = total.astype(BF)
            return 0

        lax.fori_loop(0, NY, add, 0)
        second = [
            push(acc1.at[(y + d) % NY], yin1.at[n], b_s.at[n], b_r.at[n], ys[n])
            for n, d in enumerate(DY)
        ]
        total = acc1[y].astype(F32)
        for n, copy in enumerate(second):
            copy.wait_recv()
            total = total + yin1[n].astype(F32)
        part[...] = total
        for copy in first + second:
            copy.wait_send()

    pair = push(part.at[1 - x], x_in, x_s, x_r, mate)
    pair.wait_recv()
    chunk[...] = part[x] + x_in[...]
    last = push(chunk.at[pl.ds((1 - c) * 32, 32)], c_in, c_s, c_r, other)
    hidden.wait_recv()

    def add(n, _):
        cols = pl.ds(pl.multiple_of(n * 512, 512), 512)
        gh[:, cols] = (ph[:, cols].astype(F32) + h_in[:, cols].astype(F32)).astype(BF)
        return 0

    lax.fori_loop(0, 8, add, 0)
    last.wait_recv()

    @pl.when(c == 0)
    def _():
        gk[:, 0:HD] = chunk[0:32, 0:HD]
        gv[:, 0:HD] = chunk[0:32, HD : 2 * HD]
        gk[:, HD : 2 * HD] = c_in[:, 0:HD]
        gv[:, HD : 2 * HD] = c_in[:, HD : 2 * HD]

    @pl.when(c == 1)
    def _():
        gk[:, 0:HD] = c_in[:, 0:HD]
        gv[:, 0:HD] = c_in[:, HD : 2 * HD]
        gk[:, HD : 2 * HD] = chunk[32:64, 0:HD]
        gv[:, HD : 2 * HD] = chunk[32:64, HD : 2 * HD]

    last.wait_send()
    pair.wait_send()
    hidden.wait_send()


def sum_up(ph, wg):
    dma = pltpu.SemaphoreType.DMA
    return pl.pallas_call(
        sums_kernel,
        out_shape=(
            jax.ShapeDtypeStruct((128, 4096), BF),
            jax.ShapeDtypeStruct((32, 256), F32),
            jax.ShapeDtypeStruct((32, 256), F32),
        ),
        in_specs=[VM, VM],
        out_specs=(VM, VM, VM),
        scratch_shapes=[
            pltpu.VMEM((128, 4096), BF),
            pltpu.VMEM((3, NZ, 2, 64, 256), BF),
            pltpu.VMEM((NZ, 2, 64, 256), BF),
            pltpu.VMEM((7, 2, 64, 256), BF),
            pltpu.VMEM((7, NY, 2, 64, 256), BF),
            pltpu.VMEM((NY, 2, 64, 256), BF),
            pltpu.VMEM((3, 2, 64, 256), BF),
            pltpu.VMEM((2, 64, 256), F32),
            pltpu.VMEM((64, 256), F32),
            pltpu.VMEM((64, 256), F32),
            pltpu.VMEM((32, 256), F32),
            dma, dma, dma((7,)), dma((7,)), dma((7,)), dma((7,)), dma, dma, dma, dma,
        ],
        compiler_params=params(3),
        name="sums",
    )(ph, wg)


def body(hidden_in, queries, key_weight, value_weight, seg_ids, grad_out):
    i = lax.axis_index("ctx")
    c = i % 2
    w, hid2, q2, do2 = gather_weights(key_weight, value_weight, hidden_in, queries, grad_out)
    flat = w.reshape(4096, 256)
    kv = jnp.dot(hid2, flat, preferred_element_type=F32)
    positions = (i // 2) * 256 + jnp.arange(256, dtype=jnp.int32)
    frequency = 10000.0 ** (-(jnp.arange(64, dtype=F32) * 2.0 / HD))
    angles = positions.astype(F32)[:, None] * frequency[None, :]
    cosine, sine = jnp.cos(angles), jnp.sin(angles)
    cos2 = jnp.concatenate([cosine, cosine], axis=1)
    sin2 = jnp.concatenate([sine, -sine], axis=1)
    raw = kv[:, :HD]
    keys = raw * cos2 - jnp.concatenate([raw[:, 64:], raw[:, :64]], axis=1) * sin2
    kv = jnp.concatenate([keys, kv[:, HD:]], axis=1).astype(BF)
    win, wo = exchange_window(kv, w)
    seg = seg_ids.astype(F32).reshape(128, 128)
    att2, gq2, dkv = attention(q2, do2, win.reshape(2560, 256), seg)
    kvg, kvo, att, gq = return_gradients(dkv.reshape(5, 2, 256, 256), att2, gq2, cos2, sin2)
    own = lax.dynamic_slice_in_dim(kvg, c * 128, 128)
    nt = (((1,), (1,)), ((), ()))
    ph = lax.dot_general(own, flat, nt, preferred_element_type=F32) + lax.dot_general(
        kvo, wo.reshape(4096, 256), nt, preferred_element_type=F32
    )
    wg = lax.dot_general(hid2, kvg, (((0,), (0,)), ((), ())), preferred_element_type=F32)
    gh, gk, gv = sum_up(ph.astype(BF), wg.astype(BF).reshape(NY, NZ, 2, 64, 256))
    return att, gq, gh, gk, gv


def solution(mesh):
    placed = (
        P("ctx", None),
        P("ctx", "head"),
        P("ctx", "head"),
        P("ctx", "head"),
        P(),
        P("ctx", "head"),
    )
    return jax.shard_map(
        body,
        mesh=mesh,
        in_specs=placed,
        out_specs=(
            P("ctx", "head"),
            P("ctx", "head"),
            P("ctx", None),
            P("ctx", "head"),
            P("ctx", "head"),
        ),
        check_vma=False,
    )
```

time: 1190 us -> 205 us (0.17)
  waiting for transfers between devices: 841 us -> 0 us
  Pallas kernels: 0 us -> 186 us
  starting transfers between devices: 80 us -> 0 us
  matrix products: 86.1 us -> 8.62 us
  other arithmetic: 59.5 us -> 3.56 us
  blocking collectives: 47 us -> 0 us
  local copies, waits for them, and re-layouts: 28.6 us -> 4.97 us
  loops' own time: 23 us -> 0 us
  between operations: 14.4 us -> 0.82 us
    unnamed x3 -> x0, waiting for transfers between devices: 547 us -> none
    all_gather x1 -> x0, waiting for transfers between devices: 217 us -> none  [body(): full_weights = lax.all_gather(weight_pair, 'ctx', axis=0, tiled=True)]
    pallas_call x0 -> x5, Pallas kernels: none -> 186 us  [the longest x1 51.3 us: gather_weights(): pl.pallas_call(gather_kernel, out_shape=(jax.ShapeDtypeStruct((NY, NZ, 2,...]
    ppermute x33 -> x0, starting transfers between devices: 80 us -> none  [the longest x16 63.5 us: shifted(): return lax.ppermute(x, axis, pairs)]
    dot_general x121 -> x4, matrix products: 86.1 us -> 8.62 us  [the longest x1 2.93 us: body(): kv = jnp.dot(hid2, flat, preferred_element_type=F32)]
    ppermute x33 -> x0, waiting for transfers between devices: 77.2 us -> none  [the longest x17 63.8 us: shifted_2(): lax.ppermute(x, axis, [(i, (i + by) % devices) for i in range(devices)])]
    psum x1 -> x0, blocking collectives: 47 us -> none  [body(): grad_hidden = lax.psum(partial_hidden, 'head').astype(jnp.bfloat16)]
    add x43 -> x0, other arithmetic: 26.2 us -> none  [the longest x16 21.3 us: outward_turn(): return ((query_sum + query_part, moving + pair_part), None)]
  transfers between devices with their start and end apart: 35 -> 0, of which waited for: 24 -> 0; matrix products, arithmetic and copies ran while one was open for 9% -> 0% of each run, Pallas kernels for 0% -> 0%
where the time goes in v1:
time: 205 us; the launch traced here: 203 us
  Pallas kernels  186 us (91%)
  matrix products  8.62 us (4%)
  local copies, waits for them, and re-layouts  4.97 us (2%)
  other arithmetic  3.56 us (2%)
    pallas_call x1, Pallas kernels, gather_weights(): pl.pallas_call(gather_kernel, out_shape=(jax.ShapeDtypeStruct((NY, NZ, 2,...  51.3 us
    pallas_call x1, Pallas kernels, sum_up(): pl.pallas_call(sums_kernel, out_shape=(jax.ShapeDtypeStruct((128, 4096),...  47.6 us
    pallas_call x1, Pallas kernels, attention(): pl.pallas_call(attention_kernel, out_shape=(jax.ShapeDtypeStruct((256, 51...  32 us
    pallas_call x1, Pallas kernels, exchange_window(): pl.pallas_call(window_kernel, out_shape=(jax.ShapeDtypeStruct((5, 2, 256,...  27.8 us
    pallas_call x1, Pallas kernels, return_gradients(): pl.pallas_call(return_kernel, out_shape=(jax.ShapeDtypeStruct((256, 256),...  26.7 us
    unnamed x23, local copies, waits for them, and re-layouts  4.96 us

profile of v1, /device:TPU:1, one launch (start us, length us, event | category | flops | bytes accessed | tf_op | source)
XLA Modules:
  0.0 203.5 jit_solution(9017567265727726012)
XLA Ops:
  0.7 1.5 convert_bitcast_fusion.seg
  2.1 51.3 %gather.1 = (bf16[4,8,2,64,256]{4,3,2,1,0:T(8,128)(2,1)}, bf16[256,4096]{1,0:T(8,128)(2,1)}, bf16[256,512]{1,0:T(8,128)(2,1)}, bf16[256,512]{1,0:T(8,128)(2,1)}) custom-call(bf16[32,256]{1,0:T(8,128)(2,1)} %wk.1, bf16[32,256]{1,0:T(8,128)(2,1)} %wv.1, bf16[128,4096]{1,0:T(8,128)(2,1)} %hid.1, bf16[128,1024]{1,0:T(8,128)(2,1)} %q.1, bf16[128,1024]{1,0:T(8,128)(2,1)} %do.1), custom_call_target="tpu_custom_call" | custom-call | tf_op jit(solution)/shard_map/gather/pallas_call | solution.py:167
  53.5 2.9 %fusion.8 = f32[256,256]{1,0:T(8,128)S(1)} fusion(bf16[256,4096]{1,0:T(8,128)(2,1)} %get-tuple-element.23, bf16[4096,256]{1,0:T(8,128)(2,1)} %bitcast.14), kind=kOutput, calls=%fused_computation.21 | convolution fusion | flops 536870912 | bytes 4456448 | tf_op jit(solution)/shard_map/dot_general | solution.py:610
  56.4 0.5 multiply_sine_fusion
  57.0 0.9 fusion.2
  57.9 0.7 pad_maximum_fusion.2.kv
  58.5 27.8 %window.1 = (bf16[5,2,256,256]{3,2,1,0:T(8,128)(2,1)}, bf16[4,8,2,64,256]{4,3,2,1,0:T(8,128)(2,1)}) custom-call(bf16[256,256]{1,0:T(8,128)(2,1)} %pad_maximum_fusion.2.kv, bf16[4,8,2,64,256]{4,3,2,1,0:T(8,128)(2,1)} %get-tuple-element.24.w), custom_call_target="tpu_custom_call" | custom-call | tf_op jit(solution)/shard_map/window/pallas_call | solution.py:240
  86.4 0.0 copy-start
  86.4 32.0 %attention.1 = (bf16[256,512]{1,0:T(8,128)(2,1)}, bf16[256,512]{1,0:T(8,128)(2,1)}, bf16[2560,256]{1,0:T(8,128)(2,1)}) custom-call(bf16[256,512]{1,0:T(8,128)(2,1)} %get-tuple-element.21.q2, bf16[256,512]{1,0:T(8,128)(2,1)} %get-tuple-element.22.do2, bf16[2560,256]{1,0:T(8,128)(2,1)} %bitcast.19, f32[128,128]{1,0:T(8,128)} %convert_bitcast_fusion.seg), custom_call_target="tpu_custom_call" | custom-call | tf_op jit(solution)/shard_map/attention/pallas_call | solution.py:344
  118.4 26.7 %returns.1 = (bf16[256,256]{1,0:T(8,128)(2,1)}, bf16[128,256]{1,0:T(8,128)(2,1)}, bf16[128,1024]{1,0:T(8,128)(2,1)}, bf16[128,1024]{1,0:T(8,128)(2,1)}) custom-call(bf16[5,2,256,256]{3,2,1,0:T(8,128)(2,1)} %bitcast.18, bf16[256,512]{1,0:T(8,128)(2,1)} %get-tuple-element.27.att2, bf16[256,512]{1,0:T(8,128)(2,1)} %get-tuple-element.28.gq2, ...), custom_call_target="tpu_custom_call" | custom-call | tf_op jit(solution)/shard_map/returns/pallas_call | solution.py:442
  145.1 0.0 copy-done
  145.1 0.0 copy-start.1
  145.1 0.0 copy-start.3
  145.2 1.8 fusion.3
  147.0 0.0 copy-done.1
  147.0 0.0 copy-done.3
  147.0 0.0 copy-start.2
  147.0 0.0 copy-start.6
  147.0 2.1 %convolution_convert_fusion = bf16[4096,256]{1,0:T(8,128)(2,1)} fusion(bf16[256,4096]{1,0:T(8,128)(2,1)S(1)} %copy-done.1, bf16[256,256]{1,0:T(8,128)(2,1)S(1)} %copy-done.3), kind=kOutput, calls=%fused_computation | convolution fusion | flops 537919488 | bytes 4325376 | tf_op jit(solution)/shard_map/dot_general | solution.py:629
  149.1 0.0 copy-done.2
  149.1 0.0 copy-done.6
  149.1 1.8 fusion.ph
  150.9 47.6 %sums.1 = (bf16[128,4096]{1,0:T(8,128)(2,1)}, f32[32,256]{1,0:T(8,128)}, f32[32,256]{1,0:T(8,128)}) custom-call(bf16[128,4096]{1,0:T(8,128)(2,1)} %fusion.ph, bf16[4,8,2,64,256]{4,3,2,1,0:T(8,128)(2,1)} %bitcast.16), custom_call_target="tpu_custom_call" | custom-call | tf_op jit(solution)/shard_map/sums/pallas_call | solution.py:577
  198.5 0.0 copy-start.8
  198.5 0.0 copy-start.7
  198.6 0.0 copy-done.5
  198.6 0.7 copy.21
  199.3 0.7 copy.22
  200.0 2.3 %copy.23 = bf16[128,4096]{1,0:T(8,128)(2,1)} copy(bf16[128,4096]{1,0:T(8,128)(2,1)} %get-tuple-element.54) | data formatting | bytes 2097152
  202.3 0.0 copy-done.8
  202.3 0.6 copy.24
  202.9 0.6 copy.25
  (7 shorter events, 0.0 us)
Async XLA Ops:
  86.4 58.8 %copy-start = (bf16[4,8,2,64,256]{4,3,2,1,0:T(8,128)(2,1)S(1)}, bf16[4,8,2,64,256]{4,3,2,1,0:T(8,128)(2,1)}, u32[]{:S(2)}) copy-start(bf16[4,8,2,64,256]{4,3,2,1,0:T(8,128)(2,1)} %get-tuple-element.24.w) | copy-start | bytes 6291460
  145.1 1.8 copy-start.1
  145.1 1.8 copy-start.3
  147.0 2.1 %copy-start.2 = (bf16[4,8,2,64,256]{4,3,2,1,0:T(8,128)(2,1)S(1)}, bf16[4,8,2,64,256]{4,3,2,1,0:T(8,128)(2,1)}, u32[]{:S(2)}) copy-start(bf16[4,8,2,64,256]{4,3,2,1,0:T(8,128)(2,1)} %get-tuple-element.33) | copy-start | bytes 6291460
  147.0 2.1 %copy-start.6 = (bf16[128,256]{1,0:T(8,128)(2,1)S(1)}, bf16[128,256]{1,0:T(8,128)(2,1)}, u32[]{:S(2)}) copy-start(bf16[128,256]{1,0:T(8,128)(2,1)} %get-tuple-element.32) | copy-start | bytes 196612
  150.9 47.7 %copy-start.5 = (bf16[128,1024]{1,0:T(8,128)(2,1)S(1)}, bf16[128,1024]{1,0:T(8,128)(2,1)}, u32[]{:S(2)}) copy-start(bf16[128,1024]{1,0:T(8,128)(2,1)} %get-tuple-element.52) | copy-start | bytes 786436
  150.9 48.4 %copy-start.4 = (bf16[128,1024]{1,0:T(8,128)(2,1)S(1)}, bf16[128,1024]{1,0:T(8,128)(2,1)}, u32[]{:S(2)}) copy-start(bf16[128,1024]{1,0:T(8,128)(2,1)} %get-tuple-element.53) | copy-start | bytes 786436
  198.5 3.7 %copy-start.8 = (f32[32,256]{1,0:T(8,128)S(1)}, f32[32,256]{1,0:T(8,128)}, u32[]{:S(2)}) copy-start(f32[32,256]{1,0:T(8,128)} %get-tuple-element.55) | copy-start | bytes 98308
  198.5 4.3 %copy-start.7 = (f32[32,256]{1,0:T(8,128)S(1)}, f32[32,256]{1,0:T(8,128)}, u32[]{:S(2)}) copy-start(f32[32,256]{1,0:T(8,128)} %get-tuple-element.56) | copy-start | bytes 98308

commit v2 on v0

v2 whole, which is shorter than its diff:
```python
import math

import jax
import jax.numpy as jnp
from jax import lax
from jax.experimental import pallas as pl
from jax.experimental.pallas import tpu as pltpu
from jax.sharding import PartitionSpec as P

HD = 128
WINDOW = 2048
NEG = -1e30
MESH = pl.DeviceIdType.MESH
VM = pl.BlockSpec(memory_space=pltpu.VMEM)
BF = jnp.bfloat16
F32 = jnp.float32
NY, NZ = 4, 8
DZ = (1, -1, 2, -2, 3, -3, 4)
DY = (1, -1, 2)
FAR = (4, 3, -3, 2, -2, 1, -1)
SCALING = 1.0 / math.sqrt(HD)
TO_EXP2 = SCALING * math.log2(math.e)
LEFT = (((0,), (0,)), ((), ()))
RIGHT = (((1,), (1,)), ((), ()))


def coords():
    i = lax.axis_index("ctx")
    return i // 32, (i // 4) % 8, (i // 2) % 2, i % 2, lax.axis_index("head")


def dev(y, z, x, c, h):
    return (((y % NY) * NZ + z % NZ) * 4 + x * 2 + c, h)


def plane_dev(p, x, c, h):
    return ((p % 32) * 4 + x * 2 + c, h)


def remote(src, dst, send, recv, to):
    return pltpu.make_async_remote_copy(
        src_ref=src, dst_ref=dst, send_sem=send, recv_sem=recv, device_id=to, device_id_type=MESH
    )


def push(src, dst, send, recv, to):
    copy = remote(src, dst, send, recv, to)
    copy.start()
    return copy


def dot(a, b):
    return jnp.dot(a, b, preferred_element_type=F32)


def part(start, size):
    return pl.ds(pl.multiple_of(start, size), size)


def kernel(
    wk, wv, hid, q, do, seg, cos, sin,
    att, gq, gh, gk, gv,
    pw, w, wo, hs, hst, qx, dx, win, qa, da, qt, dt, s, dkv, att2, gq2,
    x_in, own, z_in, kvg, kvo, wg, ph, h_in,
    buf0, acc0, zin0, plus, minus, acc1, yin1, total, f_in,
    p_s, p_r, g_s, g_r, o_s, o_r, wo_s, wo_r, wz_s, wz_r, wx_s, wx_r,
    bx_s, bx_r, bz_s, bz_r, k_s, k_r, h_s, h_r, a_s, a_r, b_s, b_r, m_s, m_r, f_s, f_r, loc,
):
    y, z, x, c, h = coords()
    p = y * NZ + z
    chip = p * 2 + x
    other = dev(y, z, x, 1 - c, h)
    mate = dev(y, z, 1 - x, c, h)
    diag = dev(y, z, 1 - x, 1 - c, h)
    peer = dev(y, z, x, c, 1 - h)
    ys = [dev(y + d, z, x, c, h) for d in DY]
    zs = [dev(y, z + d, x, c, h) for d in DZ]
    up1, down1, up2, down2, up4, down4 = [
        plane_dev(p + d, x, c, h) for d in (1, -1, 2, -2, 4, -4)
    ]
    partners = [other, mate, diag, peer, up1, down1, up2, down2, up4, down4] + ys + zs
    barrier = pltpu.get_barrier_semaphore()
    for partner in partners:
        pl.semaphore_signal(barrier, inc=1, device_id=partner, device_id_type=MESH)
    for n in range(2):
        pw[n, :, 0:HD] = wk[:, n * HD : (n + 1) * HD]
        pw[n, :, HD : 2 * HD] = wv[:, n * HD : (n + 1) * HD]
    pl.semaphore_wait(barrier, len(partners))

    def plane(yy, zz):
        return part(((yy % NY) * NZ + zz % NZ) * 128, 128)

    def piece(xx, cc):
        return part(p * 128 + xx * 64 + cc * 32, 32)

    pieces = [
        push(pw.at[1 - c], w.at[piece(x, c)], p_s.at[0], p_r.at[0], other),
        push(pw.at[c], w.at[piece(x, c)], p_s.at[1], p_r.at[1], mate),
        push(pw.at[1 - c], w.at[piece(x, c)], p_s.at[2], p_r.at[2], diag),
    ]
    w[piece(x, c), :] = pw[c]
    theirs = part((1 - c) * 512, 512)
    mine = part(c * 512, 512)
    toks = part(c * 128, 128)
    trades = [
        push(q.at[:, theirs], qx, o_s.at[0], o_r.at[0], other),
        push(do.at[:, theirs], dx, o_s.at[1], o_r.at[1], other),
        push(hid, hs.at[toks], o_s.at[2], o_r.at[2], other),
    ]
    for copy in pieces:
        copy.wait_recv()

    def plane_sem(yy, zz):
        return g_r.at[(yy % NY) * NZ + zz % NZ]

    def wait_plane(yy, zz):
        ref = w.at[plane(yy, zz)]
        remote(ref, ref, g_s.at[0], plane_sem(yy, zz), other).wait_recv()

    def keep_own():
        def copy_rows(n, _):
            cols = part(n * 512, 512)
            hs[toks, cols] = hid[:, cols]
            return 0

        lax.fori_loop(0, 8, copy_rows, 0)

    @pl.when(c == 0)
    def _():
        sent = []

        def go(yy, zz, to):
            ref = w.at[plane(yy, zz)]
            sent.append(push(ref, ref, g_s.at[len(sent)], plane_sem(yy, zz), to))

        for n in range(4):
            go(y, z, zs[n])
        for to in ys:
            go(y, z, to)
        keep_own()
        for d in DZ:
            wait_plane(y, z + d)
            if d == 2:
                go(y, z + 2, zs[1])
            if d == -2:
                go(y, z - 2, zs[0])
                go(y, z - 2, zs[2])
            for to in ys:
                go(y, z + d, to)
        for d in (0,) + DZ:
            for e in DY:
                wait_plane(y + e, z + d)
        for copy in sent:
            copy.wait_send()

    @pl.when(c == 1)
    def _():
        sent = []

        def go(yy, zz, to):
            ref = w.at[plane(yy, zz)]
            sent.append(push(ref, ref, g_s.at[len(sent)], plane_sem(yy, zz), to))

        for to in ys:
            go(y, z, to)
        up, down = zs[0], zs[1]
        for d in range(4):
            for n, e in enumerate((0,) + DY):
                if d == 0:
                    if e:
                        wait_plane(y + e, z)
                    go(y + e, z, up)
                    go(y + e, z, down)
                    continue
                wait_plane(y + e, z - d)
                if d < 3 or n < 2:
                    go(y + e, z - d, up)
                wait_plane(y + e, z + d)
                if d < 3 or n >= 2:
                    go(y + e, z + d, down)
            if d == 0:
                keep_own()
        for e in (0,) + DY:
            wait_plane(y + e, z + 4)
        for copy in sent:
            copy.wait_send()

    for copy in trades:
        copy.wait_recv()
    weights = push(w, wo, wo_s, wo_r, other)

    def project(n, sums):
        span = part(n * 1024, 1024)
        return sums + dot(hs[:, span], w[span, :])

    raw = lax.fori_loop(0, 4, project, jnp.zeros((256, 256), F32))

    def win_rows(k, xx):
        return part((k * 2 + xx) * 256, 256)

    def win_half(k, xx, n):
        return part((k * 2 + xx) * 256 + n * 128, 128)

    keys = raw[:, 0:HD]
    win[win_rows(4, x), 0:HD] = (keys * cos[...] - pltpu.roll(keys, 64, 1) * sin[...]).astype(BF)
    win[win_rows(4, x), HD : 2 * HD] = raw[:, HD : 2 * HD].astype(BF)

    def window_up(k, n):
        return remote(
            win.at[win_half(k, x, n)], win.at[win_half(k - 1, x, n)],
            wz_s.at[k * 2 + n], wz_r.at[(k - 1) * 2 + n], up1,
        )

    def window_across(k, n):
        j = (4 - x - k) * 2 + n
        ref = win.at[win_half(k, x, n)]
        return remote(ref, ref, wx_s.at[j], wx_r.at[j], mate)

    for n in range(2):
        window_up(4, n).start()

    @pl.when(x == 0)
    def _():
        for n in range(2):
            window_across(4, n).start()

    for t in range(2):
        @pl.when(c == t)
        def _():
            for g in range(4):
                cols = pl.ds((t * 4 + g) * HD, HD)
                rows = pl.ds((t * 4 + g) * HD, HD)
                qa[rows, :] = q[:, cols]
                da[rows, :] = do[:, cols]

        @pl.when(c != t)
        def _():
            for g in range(4):
                rows = pl.ds((t * 4 + g) * HD, HD)
                qa[rows, :] = qx[:, g * HD : (g + 1) * HD]
                da[rows, :] = dx[:, g * HD : (g + 1) * HD]

    for n in range(8):
        block = slice(n * HD, (n + 1) * HD)
        qt[:, block] = qa[block, :].T
        dt[:, block] = da[block, :].T
    base = x * 256
    row = lax.broadcasted_iota(jnp.int32, (256, 128), 0)
    col = lax.broadcasted_iota(jnp.int32, (256, 128), 1)
    tilt = col - row

    def key_rows(b):
        return part(base + b * 256, 256)

    def score(b, best):
        seg_k = []
        for n in range(2):
            index = chip * 2 - 16 + b * 2 + n
            line = seg[pl.ds(jnp.maximum(index, 0), 1), :].astype(F32)
            line = jnp.where(index >= 0, line, -1.0)
            seg_k.append(jnp.broadcast_to(line, (128, 128)).T)
        seg_k = jnp.concatenate(seg_k, axis=0)
        bias = []
        for t in range(2):
            seg_q = seg[pl.ds(chip * 2 + t, 1), :].astype(F32)
            gap = tilt + (WINDOW + t * 128 - b * 256)
            ok = (seg_k == seg_q) & (gap >= 0) & (gap < WINDOW)
            bias += [jnp.where(ok, 0.0, NEG)] * 4
        k = win[key_rows(b), 0:HD]
        values = dot(k, qt[...]) * TO_EXP2 + jnp.concatenate(bias, axis=1)
        s[part(b * 256, 256), :] = values
        return jnp.maximum(best, jnp.max(values, axis=0, keepdims=True))

    best = score(8, jnp.full((1, 1024), NEG, F32))

    def turn_over(n, _):
        cols = part(n * 512, 512)
        hst[cols, :] = hs[:, cols].T
        return 0

    lax.fori_loop(0, 8, turn_over, 0)

    def inward(d, best):
        k = 4 - d
        for n in range(2):
            remote(
                win.at[win_half(k, x, n)], win.at[win_half(k, x, n)],
                wz_s.at[0], wz_r.at[k * 2 + n], up1,
            ).wait_recv()

            @pl.when(d < 4)
            def _():
                window_up(k, n).start()

            @pl.when((k >= 1) | (x == 1))
            def _():
                window_across(k, n).start()

        best = score(2 * k, best)
        for n in range(2):
            j = (d - 1) * 2 + n
            ref = win.at[win_half(4 + x - d, 1 - x, n)]
            remote(ref, ref, wx_s.at[j], wx_r.at[j], mate).wait_recv()
        return score(9 - 2 * d, best)

    best = lax.fori_loop(1, 5, inward, best)

    def mix(b, carry):
        sums, out = carry
        rows = part(b * 256, 256)
        e = jnp.exp2(s[rows, :] - best)
        s[rows, :] = e
        v = win[key_rows(b), HD : 2 * HD]
        out = out + lax.dot_general(v, e.astype(BF), LEFT, preferred_element_type=F32)
        return sums + jnp.sum(e, axis=0, keepdims=True), out

    sums, out = lax.fori_loop(
        0, 9, mix, (jnp.zeros((1, 1024), F32), jnp.zeros((HD, 1024), F32))
    )
    inverse = 1.0 / sums
    low = (out * inverse).astype(BF)
    delta = jnp.sum(low.astype(F32) * dt[...].astype(F32), axis=0, keepdims=True)
    for t in range(2):
        for g in range(4):
            n = t * 4 + g
            att2[t, :, g * HD : (g + 1) * HD] = low[:, n * HD : (n + 1) * HD].T
    trades.append(push(att2.at[1 - c], att.at[:, mine], o_s.at[3], o_r.at[3], other))
    keep_att = pltpu.make_async_copy(att2.at[c], att.at[:, mine], loc.at[0])
    keep_att.start()

    def give(b):
        j = (7 - b) // 2
        return remote(dkv.at[b], x_in.at[j], bx_s.at[j], bx_r.at[j], mate)

    def merge(k):
        j = 4 - x - k
        alone = (j < 0) | (j > 3)

        @pl.when(alone)
        def _():
            own[k] = dkv[2 * k]

        @pl.when(jnp.logical_not(alone))
        def _():
            remote(x_in.at[j], x_in.at[j], bx_s.at[0], bx_r.at[j], mate).wait_recv()
            own[k] = (dkv[2 * k].astype(F32) + x_in[j].astype(F32)).astype(BF)

    def give_back(k, to):
        return remote(own.at[k], z_in.at[k], bz_s.at[k], bz_r.at[k], to)

    def back(n, query_sum):
        b = jnp.where(n == 8, 8, n + 1 - 2 * (n % 2))
        rows = part(b * 256, 256)
        k = win[key_rows(b), 0:HD]
        v = win[key_rows(b), HD : 2 * HD]
        probs = s[rows, :] * inverse
        dscores = probs * (dot(v, dt[...]) - delta)
        probs = probs.astype(BF)
        dscores = dscores.astype(BF)
        dkv[b, :, 0:HD] = (dot(dscores, qa[...]) * SCALING).astype(BF)
        dkv[b, :, HD : 2 * HD] = dot(probs, da[...]).astype(BF)

        @pl.when((n % 2 == 0) & (n < 8))
        def _():
            give(b).start()

        @pl.when(n == 3)
        def _():
            merge(0)
            give_back(0, down4).start()

        @pl.when(n == 5)
        def _():
            merge(1)
            give_back(1, down1).start()

        return query_sum + lax.dot_general(k, dscores, LEFT, preferred_element_type=F32)

    query_sum = lax.fori_loop(0, 9, back, jnp.zeros((HD, 1024), F32))
    merge(3)
    give_back(3, down1).start()
    merge(2)
    remote(z_in.at[1], z_in.at[1], bz_s.at[1], bz_r.at[1], down1).wait_recv()
    own[2] = (own[2].astype(F32) + z_in[1].astype(F32)).astype(BF)
    give_back(2, down2).start()
    query_low = (query_sum * SCALING).astype(BF)
    for t in range(2):
        for g in range(4):
            n = t * 4 + g
            gq2[t, :, g * HD : (g + 1) * HD] = query_low[:, n * HD : (n + 1) * HD].T
    trades.append(push(gq2.at[1 - c], gq.at[:, mine], o_s.at[4], o_r.at[4], other))
    keep_gq = pltpu.make_async_copy(gq2.at[c], gq.at[:, mine], loc.at[1])
    keep_gq.start()
    merge(4)
    for k in (3, 0, 2):
        remote(z_in.at[k], z_in.at[k], bz_s.at[k], bz_r.at[k], down1).wait_recv()
    grads = (
        own[4].astype(F32) + z_in[3].astype(F32) + z_in[0].astype(F32) + z_in[2].astype(F32)
    )
    keys = grads[:, 0:HD]
    kvg[:, 0:HD] = (keys * cos[...] + pltpu.roll(keys, 64, 1) * sin[...]).astype(BF)
    kvg[:, HD : 2 * HD] = grads[:, HD : 2 * HD].astype(BF)
    crossing = push(kvg.at[part((1 - c) * 128, 128)], kvo, k_s, k_r, other)

    def outer(n, _):
        rows = part(n * 512, 512)
        wg[rows, :] = dot(hst[rows, :], kvg[...]).astype(BF)
        return 0

    lax.fori_loop(0, 8, outer, 0)

    @pl.when(c == 0)
    def _():
        for i, d in enumerate(FAR + (0,)):
            for n, e in enumerate(DY):
                push(
                    wg.at[plane(y + e, z + d)], buf0.at[i, n],
                    a_s.at[i * 3 + n], a_r.at[i * 3 + n], ys[n],
                )

    @pl.when(c == 1)
    def _():
        for n, e in enumerate((2, 1, -1, 0)):
            top = 4 if n < 2 else 3
            low = 3 if n < 2 else 4
            push(
                wg.at[plane(y + e, z + top)], plus.at[n, top - 1],
                a_s.at[n * 4 + top - 1], a_r.at[n * 4 + top - 1], zs[0],
            )
            push(
                wg.at[plane(y + e, z - low)], minus.at[n, low - 1],
                b_s.at[n * 4 + low - 1], b_r.at[n * 4 + low - 1], zs[1],
            )

    crossing.wait_recv()
    weights.wait_recv()

    def hidden(n, _):
        for m in range(2):
            span = part(n * 1024 + m * 512, 512)
            ph[n, :, m * 512 : (m + 1) * 512] = (
                lax.dot_general(kvg[toks, :], w[span, :], RIGHT, preferred_element_type=F32)
                + lax.dot_general(kvo[...], wo[span, :], RIGHT, preferred_element_type=F32)
            ).astype(BF)
        remote(ph.at[n], h_in.at[n], h_s.at[n], h_r.at[n], peer).start()
        return 0

    lax.fori_loop(0, 4, hidden, 0)

    @pl.when(c == 0)
    def _():
        for i, d in enumerate(FAR + (0,)):
            for n in range(3):
                ref = buf0.at[i, n]
                remote(ref, ref, a_s.at[0], a_r.at[i * 3 + n], other).wait_recv()
            value = (
                wg[plane(y, z + d), :].astype(F32)
                + buf0[i, 0].astype(F32)
                + buf0[i, 1].astype(F32)
                + buf0[i, 2].astype(F32)
            )
            if d:
                acc0[i] = value.astype(BF)
                push(acc0.at[i], zin0.at[i], b_s.at[i], b_r.at[i], zs[DZ.index(d)])
            else:
                total[...] = value
        for i in range(7):
            remote(zin0.at[i], zin0.at[i], b_s.at[0], b_r.at[i], other).wait_recv()
            total[...] += zin0[i].astype(F32)
        for i in range(8):
            for n in range(3):
                ref = buf0.at[i, n]
                remote(ref, ref, a_s.at[i * 3 + n], a_r.at[0], other).wait_send()
        for i in range(7):
            remote(zin0.at[i], zin0.at[i], b_s.at[i], b_r.at[0], other).wait_send()

    @pl.when(c == 1)
    def _():
        def step(ref, send, recv, n, m, e, sign, to):
            remote(ref.at[n, m], ref.at[n, m], send.at[0], recv.at[n * 4 + m], other).wait_recv()
            if m:
                ref[n, m] = (
                    ref[n, m].astype(F32) + wg[plane(y + e, z + sign * m), :].astype(F32)
                ).astype(BF)
                push(
                    ref.at[n, m], ref.at[n, m - 1],
                    send.at[n * 4 + m - 1], recv.at[n * 4 + m - 1], to,
                )

        for m in (3, 2, 1, 0):
            for n, e in enumerate((2, 1, -1, 0)):
                top = 4 if n < 2 else 3
                low = 3 if n < 2 else 4
                if m < top:
                    step(plus, a_s, a_r, n, m, e, 1, zs[0])
                if m < low:
                    step(minus, b_s, b_r, n, m, e, -1, zs[1])
                if m == 0:
                    value = (
                        wg[plane(y + e, z), :].astype(F32)
                        + plus[n, 0].astype(F32)
                        + minus[n, 0].astype(F32)
                    )
                    if e:
                        acc1[n] = value.astype(BF)
                        to = DY.index(e)
                        push(acc1.at[n], yin1.at[n], m_s.at[n], m_r.at[n], ys[to])
                    else:
                        total[...] = value
        for n in range(3):
            remote(yin1.at[n], yin1.at[n], m_s.at[0], m_r.at[n], other).wait_recv()
            total[...] += yin1[n].astype(F32)
        for n in range(4):
            top = 4 if n < 2 else 3
            low = 3 if n < 2 else 4
            for m in range(top):
                remote(
                    plus.at[n, m], plus.at[n, m], a_s.at[n * 4 + m], a_r.at[0], other
                ).wait_send()
            for m in range(low):
                remote(
                    minus.at[n, m], minus.at[n, m], b_s.at[n * 4 + m], b_r.at[0], other
                ).wait_send()
        for n in range(3):
            remote(yin1.at[n], yin1.at[n], m_s.at[n], m_r.at[0], other).wait_send()

    def rows_of(xx, cc):
        return part(xx * 64 + cc * 32, 32)

    finals = [
        push(total.at[rows_of(x, 1 - c)], f_in.at[0], f_s.at[0], f_r.at[0], other),
        push(total.at[rows_of(1 - x, c)], f_in.at[1], f_s.at[1], f_r.at[1], mate),
        push(total.at[rows_of(1 - x, 1 - c)], f_in.at[2], f_s.at[2], f_r.at[2], diag),
    ]

    def finish(n, _):
        remote(ph.at[n], h_in.at[n], h_s.at[n], h_r.at[n], peer).wait()
        cols = part(n * 1024, 1024)
        gh[:, cols] = (ph[n].astype(F32) + h_in[n].astype(F32)).astype(BF)
        return 0

    lax.fori_loop(0, 4, finish, 0)
    for copy in finals:
        copy.wait_recv()
    here = total[rows_of(x, c), :] + f_in[1]
    there = f_in[0] + f_in[2]
    for n in range(2):
        @pl.when(c == n)
        def _():
            for first, value in ((n, here), (1 - n, there)):
                gk[:, first * HD : (first + 1) * HD] = value[:, 0:HD]
                gv[:, first * HD : (first + 1) * HD] = value[:, HD : 2 * HD]

    for copy in pieces + trades[:3] + finals + [crossing, weights]:
        copy.wait_send()
    for copy in trades[3:]:
        copy.wait()
    keep_att.wait()
    keep_gq.wait()
    for n in range(2):
        for k in range(1, 5):
            window_up(k, n).wait_send()
        for j in range(4):
            ref = win.at[win_half(4 - x - j, x, n)]
            remote(ref, ref, wx_s.at[j * 2 + n], wx_r.at[0], mate).wait_send()
    for j in range(4):
        remote(x_in.at[j], x_in.at[j], bx_s.at[j], bx_r.at[0], mate).wait_send()
        remote(z_in.at[j], z_in.at[j], bz_s.at[j], bz_r.at[0], mate).wait_send()


def run(wk, wv, hid, q, do, seg, cos, sin):
    dma = pltpu.SemaphoreType.DMA
    shape = jax.ShapeDtypeStruct

    def bf(*dims):
        return pltpu.VMEM(dims, BF)

    def f32(*dims):
        return pltpu.VMEM(dims, F32)

    buffers = [
        bf(2, 32, 256), bf(4096, 256), bf(4096, 256), bf(256, 4096), bf(4096, 256),
        bf(128, 512), bf(128, 512), bf(2560, 256),
        bf(1024, 128), bf(1024, 128), bf(128, 1024), bf(128, 1024), f32(2304, 1024),
        bf(9, 256, 256), bf(2, 128, 512), bf(2, 128, 512),
        bf(4, 256, 256), bf(5, 256, 256), bf(4, 256, 256), bf(256, 256), bf(128, 256),
        bf(4096, 256), bf(4, 128, 1024), bf(4, 128, 1024),
        bf(8, 3, 128, 256), bf(7, 128, 256), bf(7, 128, 256),
        bf(4, 4, 128, 256), bf(4, 4, 128, 256), bf(3, 128, 256), bf(3, 128, 256),
        f32(128, 256), f32(3, 32, 256),
    ]
    counts = [3, 3, 31, 32, 5, 5, 0, 0, 10, 8, 8, 8, 4, 4, 4, 4, 0, 0, 4, 4, 24, 24, 16, 16, 3, 3, 3, 3, 2]
    return pl.pallas_call(
        kernel,
        out_shape=(
            shape((128, 1024), BF),
            shape((128, 1024), BF),
            shape((128, 4096), BF),
            shape((32, 256), F32),
            shape((32, 256), F32),
        ),
        in_specs=[VM] * 8,
        out_specs=(VM,) * 5,
        scratch_shapes=buffers + [dma((n,)) if n else dma for n in counts],
        compiler_params=pltpu.CompilerParams(
            collective_id=0, has_side_effects=True, vmem_limit_bytes=60 * 2**20
        ),
        name="layer",
    )(wk, wv, hid, q, do, seg, cos, sin)


def body(hidden_in, queries, key_weight, value_weight, seg_ids, grad_out):
    chip = lax.axis_index("ctx") // 2
    positions = chip * 256 + jnp.arange(256, dtype=jnp.int32)
    frequency = 10000.0 ** (-(jnp.arange(64, dtype=F32) * 2.0 / HD))
    angles = positions.astype(F32)[:, None] * frequency[None, :]
    cosine, sine = jnp.cos(angles), jnp.sin(angles)
    cos2 = jnp.concatenate([cosine, cosine], axis=1)
    sin2 = jnp.concatenate([sine, -sine], axis=1)
    seg = seg_ids.reshape(128, 128)
    return run(key_weight, value_weight, hidden_in, queries, grad_out, seg, cos2, sin2)


def solution(mesh):
    placed = (
        P("ctx", None),
        P("ctx", "head"),
        P("ctx", "head"),
        P("ctx", "head"),
        P(),
        P("ctx", "head"),
    )
    return jax.shard_map(
        body,
        mesh=mesh,
        in_specs=placed,
        out_specs=(
            P("ctx", "head"),
            P("ctx", "head"),
            P("ctx", None),
            P("ctx", "head"),
            P("ctx", "head"),
        ),
        check_vma=False,
    )
```

time: 1190 us -> 119 us (0.10)
  waiting for transfers between devices: 841 us -> 0 us
  Pallas kernels: 0 us -> 111 us
  matrix products: 86.1 us -> 0 us
  starting transfers between devices: 80 us -> 0 us
  other arithmetic: 59.5 us -> 1.39 us
  blocking collectives: 47 us -> 0 us
  loops' own time: 23 us -> 0 us
  local copies, waits for them, and re-layouts: 28.6 us -> 5.79 us
  between operations: 14.4 us -> 0.68 us
    unnamed x3 -> x0, waiting for transfers between devices: 547 us -> none
    all_gather x1 -> x0, waiting for transfers between devices: 217 us -> none  [body(): full_weights = lax.all_gather(weight_pair, 'ctx', axis=0, tiled=True)]
    pallas_call x0 -> x1, Pallas kernels: none -> 111 us  [run(): pl.pallas_call(kernel, out_shape=(shape((128, 1024), BF), shape((128, 102...]
    dot_general x121 -> x0, matrix products: 86.1 us -> none  [the longest x33 22.3 us: scores_of(): jnp.einsum('qkgd,lkd->kgql', query_heads, key_block, preferred_element_ty...]
    ppermute x33 -> x0, starting transfers between devices: 80 us -> none  [the longest x16 63.5 us: shifted(): return lax.ppermute(x, axis, pairs)]
    ppermute x33 -> x0, waiting for transfers between devices: 77.2 us -> none  [the longest x17 63.8 us: shifted_2(): lax.ppermute(x, axis, [(i, (i + by) % devices) for i in range(devices)])]
    psum x1 -> x0, blocking collectives: 47 us -> none  [body(): grad_hidden = lax.psum(partial_hidden, 'head').astype(jnp.bfloat16)]
    add x43 -> x0, other arithmetic: 26.2 us -> none  [the longest x16 21.3 us: outward_turn(): return ((query_sum + query_part, moving + pair_part), None)]
  transfers between devices with their start and end apart: 35 -> 0, of which waited for: 24 -> 0; matrix products, arithmetic and copies ran while one was open for 9% -> 0% of each run, Pallas kernels for 0% -> 0%
where the time goes in v2:
time: 119 us
  Pallas kernels  111 us (93%)
  local copies, waits for them, and re-layouts  5.79 us (5%)
  other arithmetic  1.39 us (1%)
    pallas_call x1, Pallas kernels, run(): pl.pallas_call(kernel, out_shape=(shape((128, 1024), BF), shape((128, 102...  111 us
    unnamed x11, local copies, waits for them, and re-layouts  5.79 us

profile of v2, /device:TPU:1, one launch (start us, length us, event | category | flops | bytes accessed | tf_op | source)
XLA Modules:
  0.0 118.6 jit_solution(3447543802206709491)
XLA Ops:
  0.7 0.5 multiply_sine_fusion
  1.2 0.8 pad_maximum_fusion
  2.1 110.8 %layer.1 = (bf16[128,1024]{1,0:T(8,128)(2,1)}, bf16[128,1024]{1,0:T(8,128)(2,1)}, bf16[128,4096]{1,0:T(8,128)(2,1)}, f32[32,256]{1,0:T(8,128)}, f32[32,256]{1,0:T(8,128)}) custom-call(bf16[32,256]{1,0:T(8,128)(2,1)} %wk.1, bf16[32,256]{1,0:T(8,128)(2,1)} %wv.1, bf16[128,4096]{1,0:T(8,128)(2,1)} %hid.1, bf16[128,1024]{1,0:T(8,128)(2,1)} %q.1, ...), custom_call_target="tpu_custom_call" | custom-call | tf_op jit(solution)/shard_map/layer/pallas_call | solution.py:593
  112.8 0.0 copy-start
  112.8 1.8 %copy.16 = bf16[128,1024]{1,0:T(8,128)(2,1)} copy(bf16[128,1024]{1,0:T(8,128)(2,1)} %get-tuple-element.15) | data formatting | bytes 524288
  114.6 1.7 %copy.17 = bf16[128,1024]{1,0:T(8,128)(2,1)} copy(bf16[128,1024]{1,0:T(8,128)(2,1)} %get-tuple-element.16) | data formatting | bytes 524288
  116.3 0.0 copy-done
  116.3 0.0 copy-start.2
  116.3 1.0 copy.18
  117.2 0.0 copy-done.2
  117.2 0.0 copy-start.1
  117.2 0.6 copy.19
  117.9 0.2 copy-done.1
  118.0 0.6 copy.20
  (2 shorter events, 0.0 us)
Async XLA Ops:
  112.8 3.4 %copy-start = (bf16[128,4096]{1,0:T(8,128)(2,1)S(1)}, bf16[128,4096]{1,0:T(8,128)(2,1)}, u32[]{:S(2)}) copy-start(bf16[128,4096]{1,0:T(8,128)(2,1)} %get-tuple-element.17) | copy-start | bytes 3145732
  116.3 1.0 copy-start.2
  117.2 0.8 copy-start.1

commit v3 on v2

--- a/solution.py
+++ b/solution.py
@@ -2,6 +2,7 @@
 
 import jax
 import jax.numpy as jnp
+import numpy as np
 from jax import lax
 from jax.experimental import pallas as pl
 from jax.experimental.pallas import tpu as pltpu
@@ -12,6 +13,7 @@
 NEG = -1e30
 MESH = pl.DeviceIdType.MESH
 VM = pl.BlockSpec(memory_space=pltpu.VMEM)
+ANY = pl.BlockSpec(memory_space=pl.ANY)
 BF = jnp.bfloat16
 F32 = jnp.float32
 NY, NZ = 4, 8
@@ -58,13 +60,13 @@
 
 
 def kernel(
-    wk, wv, hid, q, do, seg, cos, sin,
-    att, gq, gh, gk, gv,
-    pw, w, wo, hs, hst, qx, dx, win, qa, da, qt, dt, s, dkv, att2, gq2,
-    x_in, own, z_in, kvg, kvo, wg, ph, h_in,
-    buf0, acc0, zin0, plus, minus, acc1, yin1, total, f_in,
+    wk, wv, hid, q, do, seg, table,
+    att, gq, ph_out, h_in, own_out, f_in,
+    cos, sin, top, pw, w, wo, hs, hst, q_own, d_own, qx, dx, win, qa, da, qt, dt, s, dkv, att2, gq2,
+    x_in, own, z_in, kvg, kvo, wg, ph,
+    buf0, acc0, zin0, plus, minus, acc1, yin1, total,
     p_s, p_r, g_s, g_r, o_s, o_r, wo_s, wo_r, wz_s, wz_r, wx_s, wx_r,
-    bx_s, bx_r, bz_s, bz_r, k_s, k_r, h_s, h_r, a_s, a_r, b_s, b_r, m_s, m_r, f_s, f_r, loc,
+    bx_s, bx_r, bz_s, bz_r, k_s, k_r, h_s, h_r, a_s, a_r, b_s, b_r, m_s, m_r, f_s, f_r, loc, out_sem,
 ):
     y, z, x, c, h = coords()
     p = y * NZ + z
@@ -85,6 +87,22 @@
     for n in range(2):
         pw[n, :, 0:HD] = wk[:, n * HD : (n + 1) * HD]
         pw[n, :, HD : 2 * HD] = wv[:, n * HD : (n + 1) * HD]
+    theirs = part((1 - c) * 512, 512)
+    mine = part(c * 512, 512)
+    toks = part(c * 128, 128)
+    staged = [
+        pltpu.make_async_copy(q.at[:, mine], q_own, loc.at[0]),
+        pltpu.make_async_copy(do.at[:, mine], d_own, loc.at[1]),
+        pltpu.make_async_copy(hid, hs.at[toks], loc.at[2]),
+    ]
+    for copy in staged:
+        copy.start()
+    cos_a, sin_a = table[pl.ds(chip, 1), :], table[pl.ds(64 + chip, 1), :]
+    cos_b, sin_b = table[128:384, :], table[384:640, :]
+    cos[...] = cos_a * cos_b - sin_a * sin_b
+    lane = lax.broadcasted_iota(jnp.int32, (256, HD), 1)
+    angle_sin = sin_a * cos_b + cos_a * sin_b
+    sin[...] = jnp.where(lane < 64, angle_sin, -angle_sin)
     pl.semaphore_wait(barrier, len(partners))
 
     def plane(yy, zz):
@@ -99,9 +117,6 @@
         push(pw.at[1 - c], w.at[piece(x, c)], p_s.at[2], p_r.at[2], diag),
     ]
     w[piece(x, c), :] = pw[c]
-    theirs = part((1 - c) * 512, 512)
-    mine = part(c * 512, 512)
-    toks = part(c * 128, 128)
     trades = [
         push(q.at[:, theirs], qx, o_s.at[0], o_r.at[0], other),
         push(do.at[:, theirs], dx, o_s.at[1], o_r.at[1], other),
@@ -117,14 +132,6 @@
         ref = w.at[plane(yy, zz)]
         remote(ref, ref, g_s.at[0], plane_sem(yy, zz), other).wait_recv()
 
-    def keep_own():
-        def copy_rows(n, _):
-            cols = part(n * 512, 512)
-            hs[toks, cols] = hid[:, cols]
-            return 0
-
-        lax.fori_loop(0, 8, copy_rows, 0)
-
     @pl.when(c == 0)
     def _():
         sent = []
@@ -137,7 +144,6 @@
             go(y, z, zs[n])
         for to in ys:
             go(y, z, to)
-        keep_own()
         for d in DZ:
             wait_plane(y, z + d)
             if d == 2:
@@ -173,13 +179,11 @@
                     go(y + e, z, down)
                     continue
                 wait_plane(y + e, z - d)
-                if d < 3 or n < 2:
+                if d < 3 or n < 1:
                     go(y + e, z - d, up)
                 wait_plane(y + e, z + d)
-                if d < 3 or n >= 2:
+                if d < 3 or n >= 1:
                     go(y + e, z + d, down)
-            if d == 0:
-                keep_own()
         for e in (0,) + DY:
             wait_plane(y + e, z + 4)
         for copy in sent:
@@ -187,6 +191,8 @@
 
     for copy in trades:
         copy.wait_recv()
+    for copy in staged:
+        copy.wait()
     weights = push(w, wo, wo_s, wo_r, other)
 
     def project(n, sums):
@@ -198,40 +204,40 @@
     def win_rows(k, xx):
         return part((k * 2 + xx) * 256, 256)
 
-    def win_half(k, xx, n):
-        return part((k * 2 + xx) * 256 + n * 128, 128)
+    def win_piece(k, xx, n):
+        return win.at[n // 2, part((k * 2 + xx) * 256 + (n % 2) * 128, 128)]
 
     keys = raw[:, 0:HD]
-    win[win_rows(4, x), 0:HD] = (keys * cos[...] - pltpu.roll(keys, 64, 1) * sin[...]).astype(BF)
-    win[win_rows(4, x), HD : 2 * HD] = raw[:, HD : 2 * HD].astype(BF)
+    win[0, win_rows(4, x), :] = (keys * cos[...] - pltpu.roll(keys, 64, 1) * sin[...]).astype(BF)
+    win[1, win_rows(4, x), :] = raw[:, HD : 2 * HD].astype(BF)
 
     def window_up(k, n):
         return remote(
-            win.at[win_half(k, x, n)], win.at[win_half(k - 1, x, n)],
-            wz_s.at[k * 2 + n], wz_r.at[(k - 1) * 2 + n], up1,
+            win_piece(k, x, n), win_piece(k - 1, x, n),
+            wz_s.at[k * 4 + n], wz_r.at[(k - 1) * 4 + n], up1,
         )
 
     def window_across(k, n):
-        j = (4 - x - k) * 2 + n
-        ref = win.at[win_half(k, x, n)]
+        j = (4 - x - k) * 4 + n
+        ref = win_piece(k, x, n)
         return remote(ref, ref, wx_s.at[j], wx_r.at[j], mate)
 
-    for n in range(2):
+    for n in range(4):
         window_up(4, n).start()
 
     @pl.when(x == 0)
     def _():
-        for n in range(2):
+        for n in range(4):
             window_across(4, n).start()
 
     for t in range(2):
         @pl.when(c == t)
         def _():
             for g in range(4):
-                cols = pl.ds((t * 4 + g) * HD, HD)
+                cols = pl.ds(g * HD, HD)
                 rows = pl.ds((t * 4 + g) * HD, HD)
-                qa[rows, :] = q[:, cols]
-                da[rows, :] = do[:, cols]
+                qa[rows, :] = q_own[:, cols]
+                da[rows, :] = d_own[:, cols]
 
         @pl.when(c != t)
         def _():
@@ -252,7 +258,8 @@
     def key_rows(b):
         return part(base + b * 256, 256)
 
-    def score(b, best):
+    def forward(b, carry):
+        best, sums, out = carry
         seg_k = []
         for n in range(2):
             index = chip * 2 - 16 + b * 2 + n
@@ -266,12 +273,16 @@
             gap = tilt + (WINDOW + t * 128 - b * 256)
             ok = (seg_k == seg_q) & (gap >= 0) & (gap < WINDOW)
             bias += [jnp.where(ok, 0.0, NEG)] * 4
-        k = win[key_rows(b), 0:HD]
-        values = dot(k, qt[...]) * TO_EXP2 + jnp.concatenate(bias, axis=1)
-        s[part(b * 256, 256), :] = values
-        return jnp.maximum(best, jnp.max(values, axis=0, keepdims=True))
-
-    best = score(8, jnp.full((1, 1024), NEG, F32))
+        values = dot(win[0, key_rows(b), :], qt[...]) * TO_EXP2 + jnp.concatenate(bias, axis=1)
+        higher = jnp.maximum(best, jnp.max(values, axis=0, keepdims=True))
+        e = jnp.exp2(values - higher)
+        s[part(b * 256, 256), :] = e
+        top[pl.ds(b, 1), :] = higher
+        shrink = jnp.exp2(best - higher)
+        mixed = lax.dot_general(
+            win[1, key_rows(b), :], e.astype(BF), LEFT, preferred_element_type=F32
+        )
+        return higher, sums * shrink + jnp.sum(e, axis=0, keepdims=True), out * shrink + mixed
 
     def turn_over(n, _):
         cols = part(n * 512, 512)
@@ -280,13 +291,17 @@
 
     lax.fori_loop(0, 8, turn_over, 0)
 
-    def inward(d, best):
+    def wait_mate(d):
+        for n in range(4):
+            j = (d - 1) * 4 + n
+            ref = win_piece(4 + x - d, 1 - x, n)
+            remote(ref, ref, wx_s.at[j], wx_r.at[j], mate).wait_recv()
+
+    def inward(d, carry):
         k = 4 - d
-        for n in range(2):
-            remote(
-                win.at[win_half(k, x, n)], win.at[win_half(k, x, n)],
-                wz_s.at[0], wz_r.at[k * 2 + n], up1,
-            ).wait_recv()
+        for n in range(4):
+            ref = win_piece(k, x, n)
+            remote(ref, ref, wz_s.at[0], wz_r.at[k * 4 + n], up1).wait_recv()
 
             @pl.when(d < 4)
             def _():
@@ -296,27 +311,19 @@
             def _():
                 window_across(k, n).start()
 
-        best = score(2 * k, best)
-        for n in range(2):
-            j = (d - 1) * 2 + n
-            ref = win.at[win_half(4 + x - d, 1 - x, n)]
-            remote(ref, ref, wx_s.at[j], wx_r.at[j], mate).wait_recv()
-        return score(9 - 2 * d, best)
-
-    best = lax.fori_loop(1, 5, inward, best)
-
-    def mix(b, carry):
-        sums, out = carry
-        rows = part(b * 256, 256)
-        e = jnp.exp2(s[rows, :] - best)
-        s[rows, :] = e
-        v = win[key_rows(b), HD : 2 * HD]
-        out = out + lax.dot_general(v, e.astype(BF), LEFT, preferred_element_type=F32)
-        return sums + jnp.sum(e, axis=0, keepdims=True), out
-
-    sums, out = lax.fori_loop(
-        0, 9, mix, (jnp.zeros((1, 1024), F32), jnp.zeros((HD, 1024), F32))
+        @pl.when(d > 1)
+        def _():
+            wait_mate(d - 1)
+
+        carry = forward(jnp.where(d == 1, 8, 11 - 2 * d), carry)
+        return forward(2 * k, carry)
+
+    carry = (
+        jnp.full((1, 1024), NEG, F32), jnp.zeros((1, 1024), F32), jnp.zeros((HD, 1024), F32)
     )
+    carry = lax.fori_loop(1, 5, inward, carry)
+    wait_mate(4)
+    best, sums, out = forward(1, carry)
     inverse = 1.0 / sums
     low = (out * inverse).astype(BF)
     delta = jnp.sum(low.astype(F32) * dt[...].astype(F32), axis=0, keepdims=True)
@@ -325,7 +332,7 @@
             n = t * 4 + g
             att2[t, :, g * HD : (g + 1) * HD] = low[:, n * HD : (n + 1) * HD].T
     trades.append(push(att2.at[1 - c], att.at[:, mine], o_s.at[3], o_r.at[3], other))
-    keep_att = pltpu.make_async_copy(att2.at[c], att.at[:, mine], loc.at[0])
+    keep_att = pltpu.make_async_copy(att2.at[c], att.at[:, mine], out_sem.at[0])
     keep_att.start()
 
     def give(b):
@@ -351,9 +358,9 @@
     def back(n, query_sum):
         b = jnp.where(n == 8, 8, n + 1 - 2 * (n % 2))
         rows = part(b * 256, 256)
-        k = win[key_rows(b), 0:HD]
-        v = win[key_rows(b), HD : 2 * HD]
-        probs = s[rows, :] * inverse
+        k = win[0, key_rows(b), :]
+        v = win[1, key_rows(b), :]
+        probs = s[rows, :] * (inverse * jnp.exp2(top[pl.ds(b, 1), :] - best))
         dscores = probs * (dot(v, dt[...]) - delta)
         probs = probs.astype(BF)
         dscores = dscores.astype(BF)
@@ -389,9 +396,21 @@
             n = t * 4 + g
             gq2[t, :, g * HD : (g + 1) * HD] = query_low[:, n * HD : (n + 1) * HD].T
     trades.append(push(gq2.at[1 - c], gq.at[:, mine], o_s.at[4], o_r.at[4], other))
-    keep_gq = pltpu.make_async_copy(gq2.at[c], gq.at[:, mine], loc.at[1])
+    keep_gq = pltpu.make_async_copy(gq2.at[c], gq.at[:, mine], out_sem.at[1])
     keep_gq.start()
     merge(4)
+    for n in range(4):
+        for k in range(1, 5):
+            window_up(k, n).wait_send()
+        for j in range(4):
+            ref = win_piece(4 - x - j, x, n)
+            remote(ref, ref, wx_s.at[j * 4 + n], wx_r.at[0], mate).wait_send()
+    for copy in pieces + trades[:3] + [weights]:
+        copy.wait_send()
+    for copy in trades[3:]:
+        copy.wait()
+    keep_att.wait()
+    keep_gq.wait()
     for k in (3, 0, 2):
         remote(z_in.at[k], z_in.at[k], bz_s.at[k], bz_r.at[k], down1).wait_recv()
     grads = (
@@ -443,6 +462,7 @@
                 + lax.dot_general(kvo[...], wo[span, :], RIGHT, preferred_element_type=F32)
             ).astype(BF)
         remote(ph.at[n], h_in.at[n], h_s.at[n], h_r.at[n], peer).start()
+        pltpu.make_async_copy(ph.at[n], ph_out.at[n], out_sem.at[2 + n]).start()
         return 0
 
     lax.fori_loop(0, 4, hidden, 0)
@@ -467,12 +487,6 @@
         for i in range(7):
             remote(zin0.at[i], zin0.at[i], b_s.at[0], b_r.at[i], other).wait_recv()
             total[...] += zin0[i].astype(F32)
-        for i in range(8):
-            for n in range(3):
-                ref = buf0.at[i, n]
-                remote(ref, ref, a_s.at[i * 3 + n], a_r.at[0], other).wait_send()
-        for i in range(7):
-            remote(zin0.at[i], zin0.at[i], b_s.at[i], b_r.at[0], other).wait_send()
 
     @pl.when(c == 1)
     def _():
@@ -510,6 +524,34 @@
         for n in range(3):
             remote(yin1.at[n], yin1.at[n], m_s.at[0], m_r.at[n], other).wait_recv()
             total[...] += yin1[n].astype(F32)
+
+    def rows_of(xx, cc):
+        return part(xx * 64 + cc * 32, 32)
+
+    finals = [
+        push(total.at[rows_of(x, 1 - c)], f_in.at[0], f_s.at[0], f_r.at[0], other),
+        push(total.at[rows_of(1 - x, c)], f_in.at[1], f_s.at[1], f_r.at[1], mate),
+        push(total.at[rows_of(1 - x, 1 - c)], f_in.at[2], f_s.at[2], f_r.at[2], diag),
+    ]
+
+    keep_own = pltpu.make_async_copy(total.at[rows_of(x, c)], own_out, out_sem.at[6])
+    keep_own.start()
+    crossing.wait_send()
+    for j in range(4):
+        remote(x_in.at[j], x_in.at[j], bx_s.at[j], bx_r.at[0], mate).wait_send()
+        remote(z_in.at[j], z_in.at[j], bz_s.at[j], bz_r.at[0], mate).wait_send()
+
+    @pl.when(c == 0)
+    def _():
+        for i in range(8):
+            for n in range(3):
+                ref = buf0.at[i, n]
+                remote(ref, ref, a_s.at[i * 3 + n], a_r.at[0], other).wait_send()
+        for i in range(7):
+            remote(zin0.at[i], zin0.at[i], b_s.at[i], b_r.at[0], other).wait_send()
+
+    @pl.when(c == 1)
+    def _():
         for n in range(4):
             top = 4 if n < 2 else 3
             low = 3 if n < 2 else 4
@@ -524,25 +566,62 @@
         for n in range(3):
             remote(yin1.at[n], yin1.at[n], m_s.at[n], m_r.at[0], other).wait_send()
 
-    def rows_of(xx, cc):
-        return part(xx * 64 + cc * 32, 32)
-
-    finals = [
-        push(total.at[rows_of(x, 1 - c)], f_in.at[0], f_s.at[0], f_r.at[0], other),
-        push(total.at[rows_of(1 - x, c)], f_in.at[1], f_s.at[1], f_r.at[1], mate),
-        push(total.at[rows_of(1 - x, 1 - c)], f_in.at[2], f_s.at[2], f_r.at[2], diag),
+    for copy in finals:
+        copy.wait()
+    keep_own.wait()
+    for n in range(4):
+        remote(ph.at[n], h_in.at[n], h_s.at[n], h_r.at[n], peer).wait()
+        pltpu.make_async_copy(ph.at[n], ph_out.at[n], out_sem.at[2 + n]).wait()
+
+
+def run(wk, wv, hid, q, do, seg, table):
+    dma = pltpu.SemaphoreType.DMA
+    shape = jax.ShapeDtypeStruct
+
+    def bf(*dims):
+        return pltpu.VMEM(dims, BF)
+
+    def f32(*dims):
+        return pltpu.VMEM(dims, F32)
+
+    buffers = [
+        f32(256, 128), f32(256, 128), f32(16, 1024),
+        bf(2, 32, 256), bf(4096, 256), bf(4096, 256), bf(256, 4096), bf(4096, 256),
+        bf(128, 512), bf(128, 512), bf(128, 512), bf(128, 512), bf(2, 2560, 128),
+        bf(1024, 128), bf(1024, 128), bf(128, 1024), bf(128, 1024), f32(2304, 1024),
+        bf(9, 256, 256), bf(2, 128, 512), bf(2, 128, 512),
+        bf(4, 256, 256), bf(5, 256, 256), bf(4, 256, 256), bf(256, 256), bf(128, 256),
+        bf(4096, 256), bf(4, 128, 1024),
+        bf(8, 3, 128, 256), bf(7, 128, 256), bf(7, 128, 256),
+        bf(4, 4, 128, 256), bf(4, 4, 128, 256), bf(3, 128, 256), bf(3, 128, 256),
+        f32(128, 256),
     ]
-
-    def finish(n, _):
-        remote(ph.at[n], h_in.at[n], h_s.at[n], h_r.at[n], peer).wait()
-        cols = part(n * 1024, 1024)
-        gh[:, cols] = (ph[n].astype(F32) + h_in[n].astype(F32)).astype(BF)
-        return 0
-
-    lax.fori_loop(0, 4, finish, 0)
-    for copy in finals:
-        copy.wait_recv()
-    here = total[rows_of(x, c), :] + f_in[1]
+    counts = [3, 3, 31, 32, 5, 5, 0, 0, 20, 16, 16, 16, 4, 4, 4, 4, 0, 0, 4, 4, 24, 24, 16, 16, 3, 3, 3, 3, 3, 7]
+    return pl.pallas_call(
+        kernel,
+        out_shape=(
+            shape((128, 1024), BF),
+            shape((128, 1024), BF),
+            shape((4, 128, 1024), BF),
+            shape((4, 128, 1024), BF),
+            shape((32, 256), F32),
+            shape((3, 32, 256), F32),
+        ),
+        in_specs=[VM, VM, ANY, ANY, ANY, VM, VM],
+        out_specs=(ANY,) * 6,
+        scratch_shapes=buffers + [dma((n,)) if n else dma for n in counts],
+        compiler_params=pltpu.CompilerParams(
+            collective_id=0, has_side_effects=True, vmem_limit_bytes=60 * 2**20
+        ),
+        name="layer",
+    )(wk, wv, hid, q, do, seg, table)
+
+
+def last_kernel(att_in, gq_in, ph, h_in, own, f_in, att, gq, gh, gk, gv):
+    att[...] = att_in[...]
+    gq[...] = gq_in[...]
+    c = lax.axis_index("ctx") % 2
+    here = own[...] + f_in[1]
     there = f_in[0] + f_in[2]
     for n in range(2):
         @pl.when(c == n)
@@ -551,47 +630,16 @@
                 gk[:, first * HD : (first + 1) * HD] = value[:, 0:HD]
                 gv[:, first * HD : (first + 1) * HD] = value[:, HD : 2 * HD]
 
-    for copy in pieces + trades[:3] + finals + [crossing, weights]:
-        copy.wait_send()
-    for copy in trades[3:]:
-        copy.wait()
-    keep_att.wait()
-    keep_gq.wait()
-    for n in range(2):
-        for k in range(1, 5):
-            window_up(k, n).wait_send()
-        for j in range(4):
-            ref = win.at[win_half(4 - x - j, x, n)]
-            remote(ref, ref, wx_s.at[j * 2 + n], wx_r.at[0], mate).wait_send()
-    for j in range(4):
-        remote(x_in.at[j], x_in.at[j], bx_s.at[j], bx_r.at[0], mate).wait_send()
-        remote(z_in.at[j], z_in.at[j], bz_s.at[j], bz_r.at[0], mate).wait_send()
-
-
-def run(wk, wv, hid, q, do, seg, cos, sin):
-    dma = pltpu.SemaphoreType.DMA
+    for n in range(4):
+        gh[:, n * 1024 : (n + 1) * 1024] = (
+            ph[n].astype(F32) + h_in[n].astype(F32)
+        ).astype(BF)
+
+
+def last(*parts):
     shape = jax.ShapeDtypeStruct
-
-    def bf(*dims):
-        return pltpu.VMEM(dims, BF)
-
-    def f32(*dims):
-        return pltpu.VMEM(dims, F32)
-
-    buffers = [
-        bf(2, 32, 256), bf(4096, 256), bf(4096, 256), bf(256, 4096), bf(4096, 256),
-        bf(128, 512), bf(128, 512), bf(2560, 256),
-        bf(1024, 128), bf(1024, 128), bf(128, 1024), bf(128, 1024), f32(2304, 1024),
-        bf(9, 256, 256), bf(2, 128, 512), bf(2, 128, 512),
-        bf(4, 256, 256), bf(5, 256, 256), bf(4, 256, 256), bf(256, 256), bf(128, 256),
-        bf(4096, 256), bf(4, 128, 1024), bf(4, 128, 1024),
-        bf(8, 3, 128, 256), bf(7, 128, 256), bf(7, 128, 256),
-        bf(4, 4, 128, 256), bf(4, 4, 128, 256), bf(3, 128, 256), bf(3, 128, 256),
-        f32(128, 256), f32(3, 32, 256),
-    ]
-    counts = [3, 3, 31, 32, 5, 5, 0, 0, 10, 8, 8, 8, 4, 4, 4, 4, 0, 0, 4, 4, 24, 24, 16, 16, 3, 3, 3, 3, 2]
     return pl.pallas_call(
-        kernel,
+        last_kernel,
         out_shape=(
             shape((128, 1024), BF),
             shape((128, 1024), BF),
@@ -599,26 +647,24 @@
             shape((32, 256), F32),
             shape((32, 256), F32),
         ),
-        in_specs=[VM] * 8,
+        in_specs=[VM] * 6,
         out_specs=(VM,) * 5,
-        scratch_shapes=buffers + [dma((n,)) if n else dma for n in counts],
-        compiler_params=pltpu.CompilerParams(
-            collective_id=0, has_side_effects=True, vmem_limit_bytes=60 * 2**20
-        ),
-        name="layer",
-    )(wk, wv, hid, q, do, seg, cos, sin)
+        compiler_params=pltpu.CompilerParams(vmem_limit_bytes=32 * 2**20),
+        name="last",
+    )(*parts)
+
+
+def tables():
+    frequency = 10000.0 ** (-(np.arange(64) * 2.0 / HD))
+    first = (np.arange(64) * 256)[:, None] * frequency[None, :]
+    within = np.arange(256)[:, None] * frequency[None, :]
+    both = np.concatenate([np.cos(first), np.sin(first), np.cos(within), np.sin(within)])
+    return jnp.asarray(np.concatenate([both, both], axis=1), F32)
 
 
 def body(hidden_in, queries, key_weight, value_weight, seg_ids, grad_out):
-    chip = lax.axis_index("ctx") // 2
-    positions = chip * 256 + jnp.arange(256, dtype=jnp.int32)
-    frequency = 10000.0 ** (-(jnp.arange(64, dtype=F32) * 2.0 / HD))
-    angles = positions.astype(F32)[:, None] * frequency[None, :]
-    cosine, sine = jnp.cos(angles), jnp.sin(angles)
-    cos2 = jnp.concatenate([cosine, cosine], axis=1)
-    sin2 = jnp.concatenate([sine, -sine], axis=1)
     seg = seg_ids.reshape(128, 128)
-    return run(key_weight, value_weight, hidden_in, queries, grad_out, seg, cos2, sin2)
+    return last(*run(key_weight, value_weight, hidden_in, queries, grad_out, seg, tables()))
 
 
 def solution(mesh):

time: 119 us -> 114 us (0.958)
  Pallas kernels: 111 us -> 107 us
  other arithmetic: 1.39 us -> 0 us
    pallas_call x1, Pallas kernels: 111 us -> 106 us  [run(): pl.pallas_call(kernel, out_shape=(shape((128, 1024), BF), shape((128, 102...]
    pallas_call x0 -> x1, Pallas kernels: none -> 1.38 us  [last(): pl.pallas_call(last_kernel, out_shape=(shape((128, 1024), BF), shape((128...]
    unnamed x11 -> x12, local copies, waits for them, and re-layouts: 5.79 us -> 5.99 us
where the time goes in v3:
time: 114 us
  Pallas kernels  107 us (94%)
  local copies, waits for them, and re-layouts  5.99 us (5%)
    pallas_call x1, Pallas kernels, run(): pl.pallas_call(kernel, out_shape=(shape((128, 1024), BF), shape((128, 102...  106 us
    unnamed x12, local copies, waits for them, and re-layouts  5.99 us

profile of v3, /device:TPU:1, one launch (start us, length us, event | category | flops | bytes accessed | tf_op | source)
XLA Modules:
  0.0 113.6 jit_solution(10066614566934571002)
XLA Ops:
  0.6 105.6 %layer.1 = (bf16[128,1024]{1,0:T(8,128)(2,1)}, bf16[128,1024]{1,0:T(8,128)(2,1)}, bf16[4,128,1024]{2,1,0:T(8,128)(2,1)}, bf16[4,128,1024]{2,1,0:T(8,128)(2,1)}, ...) custom-call(bf16[32,256]{1,0:T(8,128)(2,1)} %wk.1, bf16[32,256]{1,0:T(8,128)(2,1)} %wv.1, bf16[128,4096]{1,0:T(8,128)(2,1)} %hid.1, ...), custom_call_target="tpu_custom_call" | custom-call | tf_op jit(solution)/shard_map/layer/pallas_call | solution.py:600
  106.3 0.0 copy-start
  106.3 1.2 %copy-done = bf16[4,128,1024]{2,1,0:T(8,128)(2,1)S(1)} copy-done((bf16[4,128,1024]{2,1,0:T(8,128)(2,1)S(1)}, bf16[4,128,1024]{2,1,0:T(8,128)(2,1)}, u32[]{:S(2)}) %copy-start) | copy-done | bytes 1048600
  107.5 0.0 copy-start.1
  107.5 1.2 %copy-done.1 = bf16[4,128,1024]{2,1,0:T(8,128)(2,1)S(1)} copy-done((bf16[4,128,1024]{2,1,0:T(8,128)(2,1)S(1)}, bf16[4,128,1024]{2,1,0:T(8,128)(2,1)}, u32[]{:S(2)}) %copy-start.1) | copy-done | bytes 1048600
  108.7 0.0 copy-start.2
  108.7 0.9 copy-done.2
  109.7 0.0 copy-start.3
  109.7 0.9 copy-done.3
  110.6 0.0 copy-start.4
  110.6 0.9 copy-done.4
  111.5 0.0 copy-start.5
  111.5 0.8 copy-done.5
  112.3 1.4 %last.1 = (bf16[128,1024]{1,0:T(8,128)(2,1)}, bf16[128,1024]{1,0:T(8,128)(2,1)}, bf16[128,4096]{1,0:T(8,128)(2,1)}, f32[32,256]{1,0:T(8,128)}, f32[32,256]{1,0:T(8,128)}) custom-call(bf16[128,1024]{1,0:T(8,128)(2,1)S(1)} %copy-done.2, bf16[128,1024]{1,0:T(8,128)(2,1)S(1)} %copy-done.3, bf16[4,128,1024]{2,1,0:T(8,128)(2,1)S(1)} %copy-done, ...), custom_call_target="tpu_custom_call" | custom-call | tf_op jit(solution)/shard_map/last/pallas_call | solution.py:641
Async XLA Ops:
  106.3 1.2 %copy-start = (bf16[4,128,1024]{2,1,0:T(8,128)(2,1)S(1)}, bf16[4,128,1024]{2,1,0:T(8,128)(2,1)}, u32[]{:S(2)}) copy-start(bf16[4,128,1024]{2,1,0:T(8,128)(2,1)} %get-tuple-element.13.ph) | copy-start | bytes 3145732
  107.5 1.2 %copy-start.1 = (bf16[4,128,1024]{2,1,0:T(8,128)(2,1)S(1)}, bf16[4,128,1024]{2,1,0:T(8,128)(2,1)}, u32[]{:S(2)}) copy-start(bf16[4,128,1024]{2,1,0:T(8,128)(2,1)} %get-tuple-element.14.h_in) | copy-start | bytes 3145732
  108.7 0.9 copy-start.2
  109.7 0.9 copy-start.3
  110.6 0.9 copy-start.4
  111.5 0.8 copy-start.5

commit v4 on v3

--- a/solution.py
+++ b/solution.py
@@ -335,28 +335,41 @@
     keep_att = pltpu.make_async_copy(att2.at[c], att.at[:, mine], out_sem.at[0])
     keep_att.start()
 
-    def give(b):
+    def rows_half(n):
+        return pl.ds(n * 128, 128)
+
+    def give(b, n):
         j = (7 - b) // 2
-        return remote(dkv.at[b], x_in.at[j], bx_s.at[j], bx_r.at[j], mate)
-
-    def merge(k):
-        j = 4 - x - k
-        alone = (j < 0) | (j > 3)
-
-        @pl.when(alone)
-        def _():
-            own[k] = dkv[2 * k]
-
-        @pl.when(jnp.logical_not(alone))
-        def _():
-            remote(x_in.at[j], x_in.at[j], bx_s.at[0], bx_r.at[j], mate).wait_recv()
-            own[k] = (dkv[2 * k].astype(F32) + x_in[j].astype(F32)).astype(BF)
-
-    def give_back(k, to):
-        return remote(own.at[k], z_in.at[k], bz_s.at[k], bz_r.at[k], to)
+        return remote(
+            dkv.at[b, rows_half(n)], x_in.at[j, rows_half(n)],
+            bx_s.at[j * 2 + n], bx_r.at[j * 2 + n], mate,
+        )
+
+    def pass_on(k, n):
+        return remote(
+            own.at[k, rows_half(n)], z_in.at[k + 1, rows_half(n)],
+            bz_s.at[k * 2 + n], bz_r.at[k * 2 + n], down1,
+        )
+
+    straight = remote(own.at[0], z_in.at[0], bz_s.at[0], bz_r.at[0], down4)
+
+    def merge(k, j, n, chain):
+        rows = rows_half(n)
+        value = dkv[2 * k, rows, :].astype(F32)
+        if j is not None:
+            ref = x_in.at[j, rows]
+            remote(ref, ref, bx_s.at[0], bx_r.at[j * 2 + n], mate).wait_recv()
+            value = value + x_in[j, rows, :].astype(F32)
+        if chain:
+            ref = z_in.at[k, rows]
+            remote(ref, ref, bz_s.at[0], bz_r.at[(k - 1) * 2 + n], down1).wait_recv()
+            value = value + z_in[k, rows, :].astype(F32)
+        own[k, rows, :] = value.astype(BF)
 
     def back(n, query_sum):
-        b = jnp.where(n == 8, 8, n + 1 - 2 * (n % 2))
+        odd = n % 2
+        b = jnp.where(n < 4, jnp.where(odd == 1, 3 - n, jnp.where(x == 0, 3 - n, n + 1)), n + 1 - 2 * odd)
+        b = jnp.where(n == 8, 8, b)
         rows = part(b * 256, 256)
         k = win[0, key_rows(b), :]
         v = win[1, key_rows(b), :]
@@ -367,29 +380,37 @@
         dkv[b, :, 0:HD] = (dot(dscores, qa[...]) * SCALING).astype(BF)
         dkv[b, :, HD : 2 * HD] = dot(probs, da[...]).astype(BF)
 
-        @pl.when((n % 2 == 0) & (n < 8))
-        def _():
-            give(b).start()
-
-        @pl.when(n == 3)
-        def _():
-            merge(0)
-            give_back(0, down4).start()
+        @pl.when((odd == 0) & (n < 8))
+        def _():
+            for half in range(2):
+                give(b, half).start()
+
+        @pl.when((n == 3) & (x == 0))
+        def _():
+            for half in range(2):
+                merge(0, None, half, False)
+            straight.start()
 
         @pl.when(n == 5)
         def _():
-            merge(1)
-            give_back(1, down1).start()
+            for half in range(2):
+                merge(1, 3 - x, half, False)
+                pass_on(1, half).start()
 
         return query_sum + lax.dot_general(k, dscores, LEFT, preferred_element_type=F32)
 
     query_sum = lax.fori_loop(0, 9, back, jnp.zeros((HD, 1024), F32))
-    merge(3)
-    give_back(3, down1).start()
-    merge(2)
-    remote(z_in.at[1], z_in.at[1], bz_s.at[1], bz_r.at[1], down1).wait_recv()
-    own[2] = (own[2].astype(F32) + z_in[1].astype(F32)).astype(BF)
-    give_back(2, down2).start()
+
+    @pl.when(x == 1)
+    def _():
+        for n in range(2):
+            merge(0, 3, n, False)
+        straight.start()
+
+    for k in (2, 3):
+        for n in range(2):
+            merge(k, 4 - x - k, n, True)
+            pass_on(k, n).start()
     query_low = (query_sum * SCALING).astype(BF)
     for t in range(2):
         for g in range(4):
@@ -398,7 +419,7 @@
     trades.append(push(gq2.at[1 - c], gq.at[:, mine], o_s.at[4], o_r.at[4], other))
     keep_gq = pltpu.make_async_copy(gq2.at[c], gq.at[:, mine], out_sem.at[1])
     keep_gq.start()
-    merge(4)
+
     for n in range(4):
         for k in range(1, 5):
             window_up(k, n).wait_send()
@@ -411,11 +432,17 @@
         copy.wait()
     keep_att.wait()
     keep_gq.wait()
-    for k in (3, 0, 2):
-        remote(z_in.at[k], z_in.at[k], bz_s.at[k], bz_r.at[k], down1).wait_recv()
-    grads = (
-        own[4].astype(F32) + z_in[3].astype(F32) + z_in[0].astype(F32) + z_in[2].astype(F32)
-    )
+    for n in range(2):
+        @pl.when(x == 0)
+        def _():
+            merge(4, 0, n, True)
+
+        @pl.when(x == 1)
+        def _():
+            merge(4, None, n, True)
+
+    straight.wait_recv()
+    grads = own[4].astype(F32) + z_in[0].astype(F32)
     keys = grads[:, 0:HD]
     kvg[:, 0:HD] = (keys * cos[...] + pltpu.roll(keys, 64, 1) * sin[...]).astype(BF)
     kvg[:, HD : 2 * HD] = grads[:, HD : 2 * HD].astype(BF)
@@ -469,6 +496,7 @@
 
     @pl.when(c == 0)
     def _():
+        ready = {4: (0, 1, 2, 3, 4), 5: (5,), 6: (6,)}
         for i, d in enumerate(FAR + (0,)):
             for n in range(3):
                 ref = buf0.at[i, n]
@@ -481,7 +509,8 @@
             )
             if d:
                 acc0[i] = value.astype(BF)
-                push(acc0.at[i], zin0.at[i], b_s.at[i], b_r.at[i], zs[DZ.index(d)])
+                for m in ready.get(i, ()):
+                    push(acc0.at[m], zin0.at[m], b_s.at[m], b_r.at[m], zs[DZ.index(FAR[m])])
             else:
                 total[...] = value
         for i in range(7):
@@ -538,8 +567,12 @@
     keep_own.start()
     crossing.wait_send()
     for j in range(4):
-        remote(x_in.at[j], x_in.at[j], bx_s.at[j], bx_r.at[0], mate).wait_send()
-        remote(z_in.at[j], z_in.at[j], bz_s.at[j], bz_r.at[0], mate).wait_send()
+        for n in range(2):
+            give(7 - 2 * j, n).wait_send()
+    for k in range(1, 4):
+        for n in range(2):
+            pass_on(k, n).wait_send()
+    straight.wait_send()
 
     @pl.when(c == 0)
     def _():
@@ -590,13 +623,13 @@
         bf(128, 512), bf(128, 512), bf(128, 512), bf(128, 512), bf(2, 2560, 128),
         bf(1024, 128), bf(1024, 128), bf(128, 1024), bf(128, 1024), f32(2304, 1024),
         bf(9, 256, 256), bf(2, 128, 512), bf(2, 128, 512),
-        bf(4, 256, 256), bf(5, 256, 256), bf(4, 256, 256), bf(256, 256), bf(128, 256),
+        bf(4, 256, 256), bf(5, 256, 256), bf(5, 256, 256), bf(256, 256), bf(128, 256),
         bf(4096, 256), bf(4, 128, 1024),
         bf(8, 3, 128, 256), bf(7, 128, 256), bf(7, 128, 256),
         bf(4, 4, 128, 256), bf(4, 4, 128, 256), bf(3, 128, 256), bf(3, 128, 256),
         f32(128, 256),
     ]
-    counts = [3, 3, 31, 32, 5, 5, 0, 0, 20, 16, 16, 16, 4, 4, 4, 4, 0, 0, 4, 4, 24, 24, 16, 16, 3, 3, 3, 3, 3, 7]
+    counts = [3, 3, 31, 32, 5, 5, 0, 0, 20, 16, 16, 16, 8, 8, 8, 8, 0, 0, 4, 4, 24, 24, 16, 16, 3, 3, 3, 3, 3, 7]
     return pl.pallas_call(
         kernel,
         out_shape=(
@@ -617,39 +650,80 @@
     )(wk, wv, hid, q, do, seg, table)
 
 
-def last_kernel(att_in, gq_in, ph, h_in, own, f_in, att, gq, gh, gk, gv):
-    att[...] = att_in[...]
-    gq[...] = gq_in[...]
+def last_kernel(
+    att_in, gq_in, ph_in, h_in, own_in, f_in, att, gq, gh, gk, gv,
+    ph, hb, at, qt, own, f, gsum, gkb, gvb, sem_in, sem_out
+):
+    def load(src, dst, n):
+        copy = pltpu.make_async_copy(src, dst, sem_in.at[n])
+        copy.start()
+        return copy
+
+    def store(src, dst, n):
+        copy = pltpu.make_async_copy(src, dst, sem_out.at[n])
+        copy.start()
+        return copy
+
+    parts = [
+        (load(ph_in.at[n], ph.at[n], n), load(h_in.at[n], hb.at[n], 4 + n)) for n in range(4)
+    ]
+    small = [load(own_in, own, 8), load(f_in, f, 9)]
+    whole = [load(att_in, at, 10), load(gq_in, qt, 11)]
+    stores = []
+    for n in range(4):
+        for copy in parts[n]:
+            copy.wait()
+        gsum[:, n * 1024 : (n + 1) * 1024] = (ph[n].astype(F32) + hb[n].astype(F32)).astype(BF)
+        cols = pl.ds(n * 1024, 1024)
+        stores.append(store(gsum.at[:, cols], gh.at[:, cols], n))
+    for n, (copy, src, dst) in enumerate(((whole[0], at, att), (whole[1], qt, gq))):
+        copy.wait()
+        stores.append(store(src, dst, 4 + n))
+    for copy in small:
+        copy.wait()
     c = lax.axis_index("ctx") % 2
-    here = own[...] + f_in[1]
-    there = f_in[0] + f_in[2]
+    here = own[...] + f[1]
+    there = f[0] + f[2]
     for n in range(2):
         @pl.when(c == n)
         def _():
             for first, value in ((n, here), (1 - n, there)):
-                gk[:, first * HD : (first + 1) * HD] = value[:, 0:HD]
-                gv[:, first * HD : (first + 1) * HD] = value[:, HD : 2 * HD]
-
-    for n in range(4):
-        gh[:, n * 1024 : (n + 1) * 1024] = (
-            ph[n].astype(F32) + h_in[n].astype(F32)
-        ).astype(BF)
+                gkb[:, first * HD : (first + 1) * HD] = value[:, 0:HD]
+                gvb[:, first * HD : (first + 1) * HD] = value[:, HD : 2 * HD]
+
+    stores += [store(gkb, gk, 6), store(gvb, gv, 7)]
+    for copy in stores:
+        copy.wait()
 
 
 def last(*parts):
-    shape = jax.ShapeDtypeStruct
+    dma = pltpu.SemaphoreType.DMA
+    results = (
+        jax.ShapeDtypeStruct((128, 1024), BF),
+        jax.ShapeDtypeStruct((128, 1024), BF),
+        jax.ShapeDtypeStruct((128, 4096), BF),
+        jax.ShapeDtypeStruct((32, 256), F32),
+        jax.ShapeDtypeStruct((32, 256), F32),
+    )
     return pl.pallas_call(
         last_kernel,
-        out_shape=(
-            shape((128, 1024), BF),
-            shape((128, 1024), BF),
-            shape((128, 4096), BF),
-            shape((32, 256), F32),
-            shape((32, 256), F32),
-        ),
-        in_specs=[VM] * 6,
-        out_specs=(VM,) * 5,
-        compiler_params=pltpu.CompilerParams(vmem_limit_bytes=32 * 2**20),
+        out_shape=results,
+        in_specs=[ANY] * 6,
+        out_specs=(ANY,) * 5,
+        scratch_shapes=[
+            pltpu.VMEM((4, 128, 1024), BF),
+            pltpu.VMEM((4, 128, 1024), BF),
+            pltpu.VMEM((128, 1024), BF),
+            pltpu.VMEM((128, 1024), BF),
+            pltpu.VMEM((32, 256), F32),
+            pltpu.VMEM((3, 32, 256), F32),
+            pltpu.VMEM((128, 4096), BF),
+            pltpu.VMEM((32, 256), F32),
+            pltpu.VMEM((32, 256), F32),
+            dma((12,)),
+            dma((8,)),
+        ],
+        compiler_params=pltpu.CompilerParams(vmem_limit_bytes=60 * 2**20),
         name="last",
     )(*parts)
 

time: 114 us -> 108 us (0.947)
  local copies, waits for them, and re-layouts: 5.99 us -> 0 us
    unnamed x12 -> x0, local copies, waits for them, and re-layouts: 5.99 us -> none
    pallas_call x1, Pallas kernels: 106 us -> 104 us  [run(): pl.pallas_call(kernel, out_shape=(shape((128, 1024), BF), shape((128, 102...]
    pallas_call x1, Pallas kernels: 1.38 us -> 2.63 us  [last(): pl.pallas_call(last_kernel, out_shape=results, in_specs=[ANY] * 6, out_sp...]
where the time goes in v4:
time: 108 us; the launch traced here: 107 us
  Pallas kernels  107 us (99%)
    pallas_call x1, Pallas kernels, run(): pl.pallas_call(kernel, out_shape=(shape((128, 1024), BF), shape((128, 102...  104 us
    pallas_call x1, Pallas kernels, last(): pl.pallas_call(last_kernel, out_shape=results, in_specs=[ANY] * 6, out_sp...  2.63 us

profile of v4, /device:TPU:1, one launch (start us, length us, event | category | flops | bytes accessed | tf_op | source)
XLA Modules:
  0.0 107.4 jit_solution(6865517122849951837)
XLA Ops:
  0.6 104.1 %layer.1 = (bf16[128,1024]{1,0:T(8,128)(2,1)}, bf16[128,1024]{1,0:T(8,128)(2,1)}, bf16[4,128,1024]{2,1,0:T(8,128)(2,1)}, bf16[4,128,1024]{2,1,0:T(8,128)(2,1)}, ...) custom-call(bf16[32,256]{1,0:T(8,128)(2,1)} %wk.1, bf16[32,256]{1,0:T(8,128)(2,1)} %wv.1, bf16[128,4096]{1,0:T(8,128)(2,1)} %hid.1, ...), custom_call_target="tpu_custom_call" | custom-call | tf_op jit(solution)/shard_map/layer/pallas_call | solution.py:633
  104.7 2.6 %last.1 = (bf16[128,1024]{1,0:T(8,128)(2,1)}, bf16[128,1024]{1,0:T(8,128)(2,1)}, bf16[128,4096]{1,0:T(8,128)(2,1)}, f32[32,256]{1,0:T(8,128)}, f32[32,256]{1,0:T(8,128)}) custom-call(bf16[128,1024]{1,0:T(8,128)(2,1)} %get-tuple-element.11.att_in, bf16[128,1024]{1,0:T(8,128)(2,1)} %get-tuple-element.12.gq_in, bf16[4,128,1024]{2,1,0:T(8,128)(2,1)} %get-tuple-element.13.ph_in, ...), custom_call_target="tpu_custom_call" | custom-call | tf_op jit(solution)/shard_map/last/pallas_call | solution.py:708

commit v5 on v4

--- a/solution.py
+++ b/solution.py
@@ -51,6 +51,10 @@
     return copy
 
 
+def all_sent(ref, sem, to):
+    remote(ref, ref, sem, sem, to).wait_send()
+
+
 def dot(a, b):
     return jnp.dot(a, b, preferred_element_type=F32)
 
@@ -64,9 +68,9 @@
     att, gq, ph_out, h_in, own_out, f_in,
     cos, sin, top, pw, w, wo, hs, hst, q_own, d_own, qx, dx, win, qa, da, qt, dt, s, dkv, att2, gq2,
     x_in, own, z_in, kvg, kvo, wg, ph,
-    buf0, acc0, zin0, plus, minus, acc1, yin1, total,
-    p_s, p_r, g_s, g_r, o_s, o_r, wo_s, wo_r, wz_s, wz_r, wx_s, wx_r,
-    bx_s, bx_r, bz_s, bz_r, k_s, k_r, h_s, h_r, a_s, a_r, b_s, b_r, m_s, m_r, f_s, f_r, loc, out_sem,
+    relay, buf0, acc0, zin0, plus, minus, acc1, yin1, total,
+    p_s, p_r, g_s, g_r, v_s, v_r, o_s, o_r, wo_s, wo_r, wz_s, wz_r, wx_s, wx_r,
+    bx_s, bx_r, bz_s, bz_r, k_s, k_r, h_s, h_r, l_r, a_s, a_r, b_s, b_r, m_s, m_r, f_s, f_r, loc, out_sem,
 ):
     y, z, x, c, h = coords()
     p = y * NZ + z
@@ -77,10 +81,8 @@
     peer = dev(y, z, x, c, 1 - h)
     ys = [dev(y + d, z, x, c, h) for d in DY]
     zs = [dev(y, z + d, x, c, h) for d in DZ]
-    up1, down1, up2, down2, up4, down4 = [
-        plane_dev(p + d, x, c, h) for d in (1, -1, 2, -2, 4, -4)
-    ]
-    partners = [other, mate, diag, peer, up1, down1, up2, down2, up4, down4] + ys + zs
+    up1, down1 = plane_dev(p + 1, x, c, h), plane_dev(p - 1, x, c, h)
+    partners = [other, mate, diag, peer, up1, down1] + ys + zs
     barrier = pltpu.get_barrier_semaphore()
     for partner in partners:
         pl.semaphore_signal(barrier, inc=1, device_id=partner, device_id_type=MESH)
@@ -112,9 +114,9 @@
         return part(p * 128 + xx * 64 + cc * 32, 32)
 
     pieces = [
-        push(pw.at[1 - c], w.at[piece(x, c)], p_s.at[0], p_r.at[0], other),
-        push(pw.at[c], w.at[piece(x, c)], p_s.at[1], p_r.at[1], mate),
-        push(pw.at[1 - c], w.at[piece(x, c)], p_s.at[2], p_r.at[2], diag),
+        push(pw.at[1 - c], w.at[piece(x, c)], p_s, p_r.at[0], other),
+        push(pw.at[c], w.at[piece(x, c)], p_s, p_r.at[1], mate),
+        push(pw.at[1 - c], w.at[piece(x, c)], p_s, p_r.at[2], diag),
     ]
     w[piece(x, c), :] = pw[c]
     trades = [
@@ -130,15 +132,13 @@
 
     def wait_plane(yy, zz):
         ref = w.at[plane(yy, zz)]
-        remote(ref, ref, g_s.at[0], plane_sem(yy, zz), other).wait_recv()
+        remote(ref, ref, g_s, plane_sem(yy, zz), other).wait_recv()
 
     @pl.when(c == 0)
     def _():
-        sent = []
-
         def go(yy, zz, to):
             ref = w.at[plane(yy, zz)]
-            sent.append(push(ref, ref, g_s.at[len(sent)], plane_sem(yy, zz), to))
+            push(ref, ref, g_s, plane_sem(yy, zz), to)
 
         for n in range(4):
             go(y, z, zs[n])
@@ -156,16 +156,24 @@
         for d in (0,) + DZ:
             for e in DY:
                 wait_plane(y + e, z + d)
-        for copy in sent:
-            copy.wait_send()
+        all_sent(w.at[pl.ds(0, 31 * 128)], g_s, other)
 
     @pl.when(c == 1)
     def _():
-        sent = []
+        def half(yy, zz):
+            return w.at[part(((yy % NY) * NZ + zz % NZ) * 128 + x * 64, 64)]
 
         def go(yy, zz, to):
-            ref = w.at[plane(yy, zz)]
-            sent.append(push(ref, ref, g_s.at[len(sent)], plane_sem(yy, zz), to))
+            ref = half(yy, zz)
+            push(ref, ref, g_s, plane_sem(yy, zz), to)
+
+        def wait_half(yy, zz):
+            ref = half(yy, zz)
+            remote(ref, ref, g_s, plane_sem(yy, zz), other).wait_recv()
+
+        def share(yy, zz):
+            ref = half(yy, zz)
+            push(ref, ref, v_s, v_r, mate)
 
         for to in ys:
             go(y, z, to)
@@ -174,20 +182,26 @@
             for n, e in enumerate((0,) + DY):
                 if d == 0:
                     if e:
-                        wait_plane(y + e, z)
+                        wait_half(y + e, z)
                     go(y + e, z, up)
                     go(y + e, z, down)
+                    if e:
+                        share(y + e, z)
                     continue
-                wait_plane(y + e, z - d)
-                if d < 3 or n < 1:
+                wait_half(y + e, z - d)
+                if d < 3 or n < 2:
                     go(y + e, z - d, up)
-                wait_plane(y + e, z + d)
-                if d < 3 or n >= 1:
+                share(y + e, z - d)
+                wait_half(y + e, z + d)
+                if d < 3 or n >= 2:
                     go(y + e, z + d, down)
+                share(y + e, z + d)
         for e in (0,) + DY:
-            wait_plane(y + e, z + 4)
-        for copy in sent:
-            copy.wait_send()
+            wait_half(y + e, z + 4)
+            share(y + e, z + 4)
+        ref = w.at[pl.ds(0, 31 * 64)]
+        remote(ref, ref, v_s, v_r, mate).wait()
+        all_sent(ref, g_s, other)
 
     for copy in trades:
         copy.wait_recv()
@@ -214,13 +228,12 @@
     def window_up(k, n):
         return remote(
             win_piece(k, x, n), win_piece(k - 1, x, n),
-            wz_s.at[k * 4 + n], wz_r.at[(k - 1) * 4 + n], up1,
+            wz_s, wz_r.at[(k - 1) * 4 + n], up1,
         )
 
     def window_across(k, n):
-        j = (4 - x - k) * 4 + n
         ref = win_piece(k, x, n)
-        return remote(ref, ref, wx_s.at[j], wx_r.at[j], mate)
+        return remote(ref, ref, wx_s, wx_r.at[4 - x - k], mate)
 
     for n in range(4):
         window_up(4, n).start()
@@ -292,16 +305,14 @@
     lax.fori_loop(0, 8, turn_over, 0)
 
     def wait_mate(d):
-        for n in range(4):
-            j = (d - 1) * 4 + n
-            ref = win_piece(4 + x - d, 1 - x, n)
-            remote(ref, ref, wx_s.at[j], wx_r.at[j], mate).wait_recv()
+        ref = win.at[:, win_rows(4 + x - d, 1 - x)]
+        remote(ref, ref, wx_s, wx_r.at[d - 1], mate).wait_recv()
 
     def inward(d, carry):
         k = 4 - d
         for n in range(4):
             ref = win_piece(k, x, n)
-            remote(ref, ref, wz_s.at[0], wz_r.at[k * 4 + n], up1).wait_recv()
+            remote(ref, ref, wz_s, wz_r.at[k * 4 + n], up1).wait_recv()
 
             @pl.when(d < 4)
             def _():
@@ -335,41 +346,39 @@
     keep_att = pltpu.make_async_copy(att2.at[c], att.at[:, mine], out_sem.at[0])
     keep_att.start()
 
-    def rows_half(n):
-        return pl.ds(n * 128, 128)
+    def rows_of_piece(n):
+        return pl.ds(n * 64, 64)
 
     def give(b, n):
         j = (7 - b) // 2
         return remote(
-            dkv.at[b, rows_half(n)], x_in.at[j, rows_half(n)],
-            bx_s.at[j * 2 + n], bx_r.at[j * 2 + n], mate,
+            dkv.at[b, rows_of_piece(n)], x_in.at[j, rows_of_piece(n)],
+            bx_s, bx_r.at[j * 4 + n], mate,
         )
 
     def pass_on(k, n):
         return remote(
-            own.at[k, rows_half(n)], z_in.at[k + 1, rows_half(n)],
-            bz_s.at[k * 2 + n], bz_r.at[k * 2 + n], down1,
+            own.at[k, rows_of_piece(n)], z_in.at[k + 1, rows_of_piece(n)],
+            bz_s, bz_r.at[k * 4 + n], down1,
         )
 
-    straight = remote(own.at[0], z_in.at[0], bz_s.at[0], bz_r.at[0], down4)
 
     def merge(k, j, n, chain):
-        rows = rows_half(n)
+        rows = rows_of_piece(n)
         value = dkv[2 * k, rows, :].astype(F32)
         if j is not None:
             ref = x_in.at[j, rows]
-            remote(ref, ref, bx_s.at[0], bx_r.at[j * 2 + n], mate).wait_recv()
+            remote(ref, ref, bx_s, bx_r.at[j * 4 + n], mate).wait_recv()
             value = value + x_in[j, rows, :].astype(F32)
         if chain:
             ref = z_in.at[k, rows]
-            remote(ref, ref, bz_s.at[0], bz_r.at[(k - 1) * 2 + n], down1).wait_recv()
+            remote(ref, ref, bz_s, bz_r.at[(k - 1) * 4 + n], down1).wait_recv()
             value = value + z_in[k, rows, :].astype(F32)
         own[k, rows, :] = value.astype(BF)
 
     def back(n, query_sum):
         odd = n % 2
-        b = jnp.where(n < 4, jnp.where(odd == 1, 3 - n, jnp.where(x == 0, 3 - n, n + 1)), n + 1 - 2 * odd)
-        b = jnp.where(n == 8, 8, b)
+        b = jnp.where(n == 8, 8, n + 1 - 2 * odd)
         rows = part(b * 256, 256)
         k = win[0, key_rows(b), :]
         v = win[1, key_rows(b), :]
@@ -382,20 +391,26 @@
 
         @pl.when((odd == 0) & (n < 8))
         def _():
-            for half in range(2):
-                give(b, half).start()
-
-        @pl.when((n == 3) & (x == 0))
-        def _():
-            for half in range(2):
-                merge(0, None, half, False)
-            straight.start()
-
-        @pl.when(n == 5)
-        def _():
-            for half in range(2):
-                merge(1, 3 - x, half, False)
-                pass_on(1, half).start()
+            for piece in range(4):
+                give(b, piece).start()
+
+        @pl.when((n == 1) & (x == 0))
+        def _():
+            for piece in range(4):
+                merge(0, None, piece, False)
+                pass_on(0, piece).start()
+
+        @pl.when((n == 6) & (x == 1))
+        def _():
+            for piece in range(4):
+                merge(0, 3, piece, False)
+                pass_on(0, piece).start()
+
+        @pl.when((n == 6) & (x == 0))
+        def _():
+            for piece in range(4):
+                merge(1, 3, piece, True)
+                pass_on(1, piece).start()
 
         return query_sum + lax.dot_general(k, dscores, LEFT, preferred_element_type=F32)
 
@@ -403,12 +418,12 @@
 
     @pl.when(x == 1)
     def _():
-        for n in range(2):
-            merge(0, 3, n, False)
-        straight.start()
+        for n in range(4):
+            merge(1, 2, n, True)
+            pass_on(1, n).start()
 
     for k in (2, 3):
-        for n in range(2):
+        for n in range(4):
             merge(k, 4 - x - k, n, True)
             pass_on(k, n).start()
     query_low = (query_sum * SCALING).astype(BF)
@@ -420,19 +435,16 @@
     keep_gq = pltpu.make_async_copy(gq2.at[c], gq.at[:, mine], out_sem.at[1])
     keep_gq.start()
 
-    for n in range(4):
-        for k in range(1, 5):
-            window_up(k, n).wait_send()
-        for j in range(4):
-            ref = win_piece(4 - x - j, x, n)
-            remote(ref, ref, wx_s.at[j * 4 + n], wx_r.at[0], mate).wait_send()
-    for copy in pieces + trades[:3] + [weights]:
+    all_sent(win.at[0, pl.ds(0, 2048)], wz_s, up1)
+    all_sent(win.at[0, pl.ds(0, 2048)], wx_s, mate)
+    all_sent(w.at[pl.ds(0, 96)], p_s, other)
+    for copy in trades[:3] + [weights]:
         copy.wait_send()
     for copy in trades[3:]:
         copy.wait()
     keep_att.wait()
     keep_gq.wait()
-    for n in range(2):
+    for n in range(4):
         @pl.when(x == 0)
         def _():
             merge(4, 0, n, True)
@@ -441,8 +453,7 @@
         def _():
             merge(4, None, n, True)
 
-    straight.wait_recv()
-    grads = own[4].astype(F32) + z_in[0].astype(F32)
+    grads = own[4].astype(F32)
     keys = grads[:, 0:HD]
     kvg[:, 0:HD] = (keys * cos[...] + pltpu.roll(keys, 64, 1) * sin[...]).astype(BF)
     kvg[:, HD : 2 * HD] = grads[:, HD : 2 * HD].astype(BF)
@@ -458,11 +469,10 @@
     @pl.when(c == 0)
     def _():
         for i, d in enumerate(FAR + (0,)):
-            for n, e in enumerate(DY):
-                push(
-                    wg.at[plane(y + e, z + d)], buf0.at[i, n],
-                    a_s.at[i * 3 + n], a_r.at[i * 3 + n], ys[n],
-                )
+            push(wg.at[plane(y + 2, z + d)], relay.at[i], a_s, l_r.at[i], ys[i % 2])
+        for i, d in enumerate(FAR + (0,)):
+            n = 1 - i % 2
+            push(wg.at[plane(y + DY[n], z + d)], buf0.at[i, n], a_s, a_r.at[i * 2 + n], ys[n])
 
     @pl.when(c == 1)
     def _():
@@ -471,11 +481,11 @@
             low = 3 if n < 2 else 4
             push(
                 wg.at[plane(y + e, z + top)], plus.at[n, top - 1],
-                a_s.at[n * 4 + top - 1], a_r.at[n * 4 + top - 1], zs[0],
+                a_s, a_r.at[n * 4 + top - 1], zs[0],
             )
             push(
                 wg.at[plane(y + e, z - low)], minus.at[n, low - 1],
-                b_s.at[n * 4 + low - 1], b_r.at[n * 4 + low - 1], zs[1],
+                b_s, b_r.at[n * 4 + low - 1], zs[1],
             )
 
     crossing.wait_recv()
@@ -496,38 +506,44 @@
 
     @pl.when(c == 0)
     def _():
+        for i, d in enumerate(FAR + (0,)):
+            n = i % 2
+            remote(relay.at[i], relay.at[i], a_s, l_r.at[i], other).wait_recv()
+            relay[i] = (
+                relay[i].astype(F32) + wg[plane(y + DY[n], z + d), :].astype(F32)
+            ).astype(BF)
+            push(relay.at[i], buf0.at[i, n], a_s, a_r.at[i * 2 + n], ys[n])
         ready = {4: (0, 1, 2, 3, 4), 5: (5,), 6: (6,)}
         for i, d in enumerate(FAR + (0,)):
-            for n in range(3):
+            for n in range(2):
                 ref = buf0.at[i, n]
-                remote(ref, ref, a_s.at[0], a_r.at[i * 3 + n], other).wait_recv()
+                remote(ref, ref, a_s, a_r.at[i * 2 + n], other).wait_recv()
             value = (
                 wg[plane(y, z + d), :].astype(F32)
                 + buf0[i, 0].astype(F32)
                 + buf0[i, 1].astype(F32)
-                + buf0[i, 2].astype(F32)
             )
             if d:
                 acc0[i] = value.astype(BF)
                 for m in ready.get(i, ()):
-                    push(acc0.at[m], zin0.at[m], b_s.at[m], b_r.at[m], zs[DZ.index(FAR[m])])
+                    push(acc0.at[m], zin0.at[m], b_s, b_r.at[m], zs[DZ.index(FAR[m])])
             else:
                 total[...] = value
         for i in range(7):
-            remote(zin0.at[i], zin0.at[i], b_s.at[0], b_r.at[i], other).wait_recv()
+            remote(zin0.at[i], zin0.at[i], b_s, b_r.at[i], other).wait_recv()
             total[...] += zin0[i].astype(F32)
 
     @pl.when(c == 1)
     def _():
         def step(ref, send, recv, n, m, e, sign, to):
-            remote(ref.at[n, m], ref.at[n, m], send.at[0], recv.at[n * 4 + m], other).wait_recv()
+            remote(ref.at[n, m], ref.at[n, m], send, recv.at[n * 4 + m], other).wait_recv()
             if m:
                 ref[n, m] = (
                     ref[n, m].astype(F32) + wg[plane(y + e, z + sign * m), :].astype(F32)
                 ).astype(BF)
                 push(
                     ref.at[n, m], ref.at[n, m - 1],
-                    send.at[n * 4 + m - 1], recv.at[n * 4 + m - 1], to,
+                    send, recv.at[n * 4 + m - 1], to,
                 )
 
         for m in (3, 2, 1, 0):
@@ -547,11 +563,11 @@
                     if e:
                         acc1[n] = value.astype(BF)
                         to = DY.index(e)
-                        push(acc1.at[n], yin1.at[n], m_s.at[n], m_r.at[n], ys[to])
+                        push(acc1.at[n], yin1.at[n], m_s, m_r.at[n], ys[to])
                     else:
                         total[...] = value
         for n in range(3):
-            remote(yin1.at[n], yin1.at[n], m_s.at[0], m_r.at[n], other).wait_recv()
+            remote(yin1.at[n], yin1.at[n], m_s, m_r.at[n], other).wait_recv()
             total[...] += yin1[n].astype(F32)
 
     def rows_of(xx, cc):
@@ -566,38 +582,19 @@
     keep_own = pltpu.make_async_copy(total.at[rows_of(x, c)], own_out, out_sem.at[6])
     keep_own.start()
     crossing.wait_send()
-    for j in range(4):
-        for n in range(2):
-            give(7 - 2 * j, n).wait_send()
-    for k in range(1, 4):
-        for n in range(2):
-            pass_on(k, n).wait_send()
-    straight.wait_send()
+    all_sent(x_in, bx_s, mate)
+    all_sent(x_in, bz_s, down1)
 
     @pl.when(c == 0)
     def _():
-        for i in range(8):
-            for n in range(3):
-                ref = buf0.at[i, n]
-                remote(ref, ref, a_s.at[i * 3 + n], a_r.at[0], other).wait_send()
-        for i in range(7):
-            remote(zin0.at[i], zin0.at[i], b_s.at[i], b_r.at[0], other).wait_send()
+        all_sent(wg.at[pl.ds(0, 24 * 128)], a_s, other)
+        all_sent(zin0, b_s, other)
 
     @pl.when(c == 1)
     def _():
-        for n in range(4):
-            top = 4 if n < 2 else 3
-            low = 3 if n < 2 else 4
-            for m in range(top):
-                remote(
-                    plus.at[n, m], plus.at[n, m], a_s.at[n * 4 + m], a_r.at[0], other
-                ).wait_send()
-            for m in range(low):
-                remote(
-                    minus.at[n, m], minus.at[n, m], b_s.at[n * 4 + m], b_r.at[0], other
-                ).wait_send()
-        for n in range(3):
-            remote(yin1.at[n], yin1.at[n], m_s.at[n], m_r.at[0], other).wait_send()
+        all_sent(wg.at[pl.ds(0, 14 * 128)], a_s, other)
+        all_sent(wg.at[pl.ds(0, 14 * 128)], b_s, other)
+        all_sent(yin1, m_s, other)
 
     for copy in finals:
         copy.wait()
@@ -625,11 +622,14 @@
         bf(9, 256, 256), bf(2, 128, 512), bf(2, 128, 512),
         bf(4, 256, 256), bf(5, 256, 256), bf(5, 256, 256), bf(256, 256), bf(128, 256),
         bf(4096, 256), bf(4, 128, 1024),
-        bf(8, 3, 128, 256), bf(7, 128, 256), bf(7, 128, 256),
+        bf(8, 128, 256), bf(8, 2, 128, 256), bf(7, 128, 256), bf(7, 128, 256),
         bf(4, 4, 128, 256), bf(4, 4, 128, 256), bf(3, 128, 256), bf(3, 128, 256),
         f32(128, 256),
     ]
-    counts = [3, 3, 31, 32, 5, 5, 0, 0, 20, 16, 16, 16, 8, 8, 8, 8, 0, 0, 4, 4, 24, 24, 16, 16, 3, 3, 3, 3, 3, 7]
+    counts = [
+        0, 3, 0, 32, 0, 0, 5, 5, 0, 0, 0, 16, 0, 4, 0, 16,
+        0, 16, 0, 0, 4, 4, 8, 0, 16, 0, 16, 0, 3, 3, 3, 3, 7,
+    ]
     return pl.pallas_call(
         kernel,
         out_shape=(

time: 108 us -> 103 us (0.954)
  Pallas kernels: 107 us -> 102 us
    pallas_call x1, Pallas kernels: 104 us -> 99.6 us  [run(): pl.pallas_call(kernel, out_shape=(shape((128, 1024), BF), shape((128, 102...]
where the time goes in v5:
time: 103 us
  Pallas kernels  102 us (99%)
    pallas_call x1, Pallas kernels, run(): pl.pallas_call(kernel, out_shape=(shape((128, 1024), BF), shape((128, 102...  99.6 us
    pallas_call x1, Pallas kernels, last(): pl.pallas_call(last_kernel, out_shape=results, in_specs=[ANY] * 6, out_sp...  2.63 us

profile of v5, /device:TPU:1, one launch (start us, length us, event | category | flops | bytes accessed | tf_op | source)
XLA Modules:
  0.0 102.9 jit_solution(6777161254807747413)
XLA Ops:
  0.6 99.6 %layer.1 = (bf16[128,1024]{1,0:T(8,128)(2,1)}, bf16[128,1024]{1,0:T(8,128)(2,1)}, bf16[4,128,1024]{2,1,0:T(8,128)(2,1)}, bf16[4,128,1024]{2,1,0:T(8,128)(2,1)}, ...) custom-call(bf16[32,256]{1,0:T(8,128)(2,1)} %wk.1, bf16[32,256]{1,0:T(8,128)(2,1)} %wv.1, bf16[128,4096]{1,0:T(8,128)(2,1)} %hid.1, ...), custom_call_target="tpu_custom_call" | custom-call | tf_op jit(solution)/shard_map/layer/pallas_call | solution.py:633
  100.3 2.6 %last.1 = (bf16[128,1024]{1,0:T(8,128)(2,1)}, bf16[128,1024]{1,0:T(8,128)(2,1)}, bf16[128,4096]{1,0:T(8,128)(2,1)}, f32[32,256]{1,0:T(8,128)}, f32[32,256]{1,0:T(8,128)}) custom-call(bf16[128,1024]{1,0:T(8,128)(2,1)} %get-tuple-element.11.att_in, bf16[128,1024]{1,0:T(8,128)(2,1)} %get-tuple-element.12.gq_in, bf16[4,128,1024]{2,1,0:T(8,128)(2,1)} %get-tuple-element.13.ph_in, ...), custom_call_target="tpu_custom_call" | custom-call | tf_op jit(solution)/shard_map/last/pallas_call | solution.py:708

commit v6 on v5

--- a/solution.py
+++ b/solution.py
@@ -19,7 +19,10 @@
 NY, NZ = 4, 8
 DZ = (1, -1, 2, -2, 3, -3, 4)
 DY = (1, -1, 2)
-FAR = (4, 3, -3, 2, -2, 1, -1)
+FAR = (4, -3, 3, -2, 2, -1, 1)
+READY = {4: (0, 1, 2, 3, 4), 5: (5,), 6: (6,)}
+LAG = 2
+AHEAD = 4
 SCALING = 1.0 / math.sqrt(HD)
 TO_EXP2 = SCALING * math.log2(math.e)
 LEFT = (((0,), (0,)), ((), ()))
@@ -64,13 +67,13 @@
 
 
 def kernel(
-    wk, wv, hid, q, do, seg, table,
+    wk, wv, hid, q, do, seg_in, table_in,
     att, gq, ph_out, h_in, own_out, f_in,
-    cos, sin, top, pw, w, wo, hs, hst, q_own, d_own, qx, dx, win, qa, da, qt, dt, s, dkv, att2, gq2,
+    seg, table, cos, sin, top, pw, w, wo, hs, hst, q_own, d_own, qx, dx, win, qa, da, qt, dt, s, dkv, att2, gq2,
     x_in, own, z_in, kvg, kvo, wg, ph,
     relay, buf0, acc0, zin0, plus, minus, acc1, yin1, total,
     p_s, p_r, g_s, g_r, v_s, v_r, o_s, o_r, wo_s, wo_r, wz_s, wz_r, wx_s, wx_r,
-    bx_s, bx_r, bz_s, bz_r, k_s, k_r, h_s, h_r, l_r, a_s, a_r, b_s, b_r, m_s, m_r, f_s, f_r, loc, out_sem,
+    bx_s, bx_r, bz_s, bz_r, k_s, k_r, h_s, h_r, l_r, a_s, a_r, b_s, b_r, m_s, m_r, f_s, f_r, loc, out_sem, in_sem,
 ):
     y, z, x, c, h = coords()
     p = y * NZ + z
@@ -86,12 +89,23 @@
     barrier = pltpu.get_barrier_semaphore()
     for partner in partners:
         pl.semaphore_signal(barrier, inc=1, device_id=partner, device_id_type=MESH)
-    for n in range(2):
-        pw[n, :, 0:HD] = wk[:, n * HD : (n + 1) * HD]
-        pw[n, :, HD : 2 * HD] = wv[:, n * HD : (n + 1) * HD]
     theirs = part((1 - c) * 512, 512)
     mine = part(c * 512, 512)
     toks = part(c * 128, 128)
+    own_weights = []
+    for n in range(2):
+        for m, ref in enumerate((wk, wv)):
+            own_weights.append(
+                pltpu.make_async_copy(
+                    ref.at[:, pl.ds(n * HD, HD)], pw.at[n, :, pl.ds(m * HD, HD)], in_sem.at[n * 2 + m]
+                )
+            )
+    small = [
+        pltpu.make_async_copy(seg_in, seg, in_sem.at[4]),
+        pltpu.make_async_copy(table_in, table, in_sem.at[5]),
+    ]
+    for copy in own_weights + small:
+        copy.start()
     staged = [
         pltpu.make_async_copy(q.at[:, mine], q_own, loc.at[0]),
         pltpu.make_async_copy(do.at[:, mine], d_own, loc.at[1]),
@@ -99,12 +113,16 @@
     ]
     for copy in staged:
         copy.start()
+    for copy in small:
+        copy.wait()
     cos_a, sin_a = table[pl.ds(chip, 1), :], table[pl.ds(64 + chip, 1), :]
     cos_b, sin_b = table[128:384, :], table[384:640, :]
     cos[...] = cos_a * cos_b - sin_a * sin_b
     lane = lax.broadcasted_iota(jnp.int32, (256, HD), 1)
     angle_sin = sin_a * cos_b + cos_a * sin_b
     sin[...] = jnp.where(lane < 64, angle_sin, -angle_sin)
+    for copy in own_weights:
+        copy.wait()
     pl.semaphore_wait(barrier, len(partners))
 
     def plane(yy, zz):
@@ -466,13 +484,20 @@
 
     lax.fori_loop(0, 8, outer, 0)
 
+    order = FAR + (0,)
+
+    def leave(i):
+        n = i % 2
+        push(wg.at[plane(y + 2, z + order[i])], relay.at[i], a_s, l_r.at[i], ys[n])
+        push(
+            wg.at[plane(y + DY[1 - n], z + order[i])], buf0.at[i, 1 - n],
+            a_s, a_r.at[i * 2 + 1 - n], ys[1 - n],
+        )
+
     @pl.when(c == 0)
     def _():
-        for i, d in enumerate(FAR + (0,)):
-            push(wg.at[plane(y + 2, z + d)], relay.at[i], a_s, l_r.at[i], ys[i % 2])
-        for i, d in enumerate(FAR + (0,)):
-            n = 1 - i % 2
-            push(wg.at[plane(y + DY[n], z + d)], buf0.at[i, n], a_s, a_r.at[i * 2 + n], ys[n])
+        for i in range(AHEAD):
+            leave(i)
 
     @pl.when(c == 1)
     def _():
@@ -506,15 +531,15 @@
 
     @pl.when(c == 0)
     def _():
-        for i, d in enumerate(FAR + (0,)):
+        def pass_row(i, d):
             n = i % 2
             remote(relay.at[i], relay.at[i], a_s, l_r.at[i], other).wait_recv()
             relay[i] = (
                 relay[i].astype(F32) + wg[plane(y + DY[n], z + d), :].astype(F32)
             ).astype(BF)
             push(relay.at[i], buf0.at[i, n], a_s, a_r.at[i * 2 + n], ys[n])
-        ready = {4: (0, 1, 2, 3, 4), 5: (5,), 6: (6,)}
-        for i, d in enumerate(FAR + (0,)):
+
+        def pass_plane(i, d):
             for n in range(2):
                 ref = buf0.at[i, n]
                 remote(ref, ref, a_s, a_r.at[i * 2 + n], other).wait_recv()
@@ -525,10 +550,18 @@
             )
             if d:
                 acc0[i] = value.astype(BF)
-                for m in ready.get(i, ()):
+                for m in READY.get(i, ()):
                     push(acc0.at[m], zin0.at[m], b_s, b_r.at[m], zs[DZ.index(FAR[m])])
             else:
                 total[...] = value
+
+        for i in range(8 + LAG):
+            if i < 8:
+                pass_row(i, order[i])
+            if i + AHEAD < 8:
+                leave(i + AHEAD)
+            if i >= LAG:
+                pass_plane(i - LAG, order[i - LAG])
         for i in range(7):
             remote(zin0.at[i], zin0.at[i], b_s, b_r.at[i], other).wait_recv()
             total[...] += zin0[i].astype(F32)
@@ -615,6 +648,7 @@
         return pltpu.VMEM(dims, F32)
 
     buffers = [
+        pltpu.VMEM((128, 128), jnp.int32), f32(640, 128),
         f32(256, 128), f32(256, 128), f32(16, 1024),
         bf(2, 32, 256), bf(4096, 256), bf(4096, 256), bf(256, 4096), bf(4096, 256),
         bf(128, 512), bf(128, 512), bf(128, 512), bf(128, 512), bf(2, 2560, 128),
@@ -628,7 +662,7 @@
     ]
     counts = [
         0, 3, 0, 32, 0, 0, 5, 5, 0, 0, 0, 16, 0, 4, 0, 16,
-        0, 16, 0, 0, 4, 4, 8, 0, 16, 0, 16, 0, 3, 3, 3, 3, 7,
+        0, 16, 0, 0, 4, 4, 8, 0, 16, 0, 16, 0, 3, 3, 3, 3, 7, 6,
     ]
     return pl.pallas_call(
         kernel,
@@ -640,7 +674,7 @@
             shape((32, 256), F32),
             shape((3, 32, 256), F32),
         ),
-        in_specs=[VM, VM, ANY, ANY, ANY, VM, VM],
+        in_specs=[ANY] * 7,
         out_specs=(ANY,) * 6,
         scratch_shapes=buffers + [dma((n,)) if n else dma for n in counts],
         compiler_params=pltpu.CompilerParams(

time: 103 us -> 104 us (level)
  no operation moved by 1% of the time
where the time goes in v6:
time: 104 us; the launch traced here: 103 us
  Pallas kernels  103 us (99%)
    pallas_call x1, Pallas kernels, run(): pl.pallas_call(kernel, out_shape=(shape((128, 1024), BF), shape((128, 102...  100 us
    pallas_call x1, Pallas kernels, last(): pl.pallas_call(last_kernel, out_shape=results, in_specs=[ANY] * 6, out_sp...  2.63 us

profile of v6, /device:TPU:1, one launch (start us, length us, event | category | flops | bytes accessed | tf_op | source)
XLA Modules:
  0.0 103.4 jit_solution(17288165557021392434)
XLA Ops:
  0.6 100.1 %layer.1 = (bf16[128,1024]{1,0:T(8,128)(2,1)}, bf16[128,1024]{1,0:T(8,128)(2,1)}, bf16[4,128,1024]{2,1,0:T(8,128)(2,1)}, bf16[4,128,1024]{2,1,0:T(8,128)(2,1)}, ...) custom-call(bf16[32,256]{1,0:T(8,128)(2,1)} %wk.1, bf16[32,256]{1,0:T(8,128)(2,1)} %wv.1, bf16[128,4096]{1,0:T(8,128)(2,1)} %hid.1, ...), custom_call_target="tpu_custom_call" | custom-call | tf_op jit(solution)/shard_map/layer/pallas_call | solution.py:667
  100.8 2.6 %last.1 = (bf16[128,1024]{1,0:T(8,128)(2,1)}, bf16[128,1024]{1,0:T(8,128)(2,1)}, bf16[128,4096]{1,0:T(8,128)(2,1)}, f32[32,256]{1,0:T(8,128)}, f32[32,256]{1,0:T(8,128)}) custom-call(bf16[128,1024]{1,0:T(8,128)(2,1)} %get-tuple-element.11.att_in, bf16[128,1024]{1,0:T(8,128)(2,1)} %get-tuple-element.12.gq_in, bf16[4,128,1024]{2,1,0:T(8,128)(2,1)} %get-tuple-element.13.ph_in, ...), custom_call_target="tpu_custom_call" | custom-call | tf_op jit(solution)/shard_map/last/pallas_call | solution.py:742

commit v7 on v6

--- a/solution.py
+++ b/solution.py
@@ -20,7 +20,7 @@
 DZ = (1, -1, 2, -2, 3, -3, 4)
 DY = (1, -1, 2)
 FAR = (4, -3, 3, -2, 2, -1, 1)
-READY = {4: (0, 1, 2, 3, 4), 5: (5,), 6: (6,)}
+READY = {2: (0, 1, 2), 3: (3,), 4: (4,), 5: (5,), 6: (6,)}
 LAG = 2
 AHEAD = 4
 SCALING = 1.0 / math.sqrt(HD)
@@ -68,11 +68,11 @@
 
 def kernel(
     wk, wv, hid, q, do, seg_in, table_in,
-    att, gq, ph_out, h_in, own_out, f_in,
-    seg, table, cos, sin, top, pw, w, wo, hs, hst, q_own, d_own, qx, dx, win, qa, da, qt, dt, s, dkv, att2, gq2,
-    x_in, own, z_in, kvg, kvo, wg, ph,
+    att, gq, gh, h_in, own_out, f_in,
+    seg, table, cos, sin, top, pw, w, wo, wp, wpo, hs, hst, q_own, d_own, qx, dx, win, qa, da, qt, dt, s, dkv, att2, gq2,
+    x_in, own, z_in, kvg, kvo, kvp, wg, ph,
     relay, buf0, acc0, zin0, plus, minus, acc1, yin1, total,
-    p_s, p_r, g_s, g_r, v_s, v_r, o_s, o_r, wo_s, wo_r, wz_s, wz_r, wx_s, wx_r,
+    p_s, p_r, g_s, g_r, v_s, v_r, q_s, q_r, o_s, o_r, wo_s, wo_r, wz_s, wz_r, wx_s, wx_r,
     bx_s, bx_r, bz_s, bz_r, k_s, k_r, h_s, h_r, l_r, a_s, a_r, b_s, b_r, m_s, m_r, f_s, f_r, loc, out_sem, in_sem,
 ):
     y, z, x, c, h = coords()
@@ -82,10 +82,11 @@
     mate = dev(y, z, 1 - x, c, h)
     diag = dev(y, z, 1 - x, 1 - c, h)
     peer = dev(y, z, x, c, 1 - h)
+    peer_other = dev(y, z, x, 1 - c, 1 - h)
     ys = [dev(y + d, z, x, c, h) for d in DY]
     zs = [dev(y, z + d, x, c, h) for d in DZ]
     up1, down1 = plane_dev(p + 1, x, c, h), plane_dev(p - 1, x, c, h)
-    partners = [other, mate, diag, peer, up1, down1] + ys + zs
+    partners = [other, mate, diag, peer, peer_other, up1, down1] + ys + zs
     barrier = pltpu.get_barrier_semaphore()
     for partner in partners:
         pl.semaphore_signal(barrier, inc=1, device_id=partner, device_id_type=MESH)
@@ -225,7 +226,15 @@
         copy.wait_recv()
     for copy in staged:
         copy.wait()
-    weights = push(w, wo, wo_s, wo_r, other)
+    weights = push(w, wo, wo_s.at[0], wo_r.at[0], other)
+
+    def lend(n):
+        return remote(
+            w.at[part((1 - h) * 1024 + n * 512, 512)], wp.at[pl.ds(n * 512, 512)],
+            q_s.at[n], q_r.at[n], peer,
+        )
+
+    lend(0).start()
 
     def project(n, sums):
         span = part(n * 1024, 1024)
@@ -412,6 +421,10 @@
             for piece in range(4):
                 give(b, piece).start()
 
+        @pl.when(n == 6)
+        def _():
+            lend(1).start()
+
         @pl.when((n == 1) & (x == 0))
         def _():
             for piece in range(4):
@@ -475,7 +488,12 @@
     keys = grads[:, 0:HD]
     kvg[:, 0:HD] = (keys * cos[...] + pltpu.roll(keys, 64, 1) * sin[...]).astype(BF)
     kvg[:, HD : 2 * HD] = grads[:, HD : 2 * HD].astype(BF)
-    crossing = push(kvg.at[part((1 - c) * 128, 128)], kvo, k_s, k_r, other)
+    away = kvg.at[part((1 - c) * 128, 128)]
+    crossing = push(away, kvo, k_s.at[0], k_r.at[0], other)
+    across = [
+        push(kvg.at[toks], kvp.at[0], k_s.at[1], k_r.at[1], peer),
+        push(away, kvp.at[1], k_s.at[2], k_r.at[2], peer_other),
+    ]
 
     def outer(n, _):
         rows = part(n * 512, 512)
@@ -518,16 +536,44 @@
 
     def hidden(n, _):
         for m in range(2):
-            span = part(n * 1024 + m * 512, 512)
+            span = part(2048 + n * 1024 + m * 512, 512)
             ph[n, :, m * 512 : (m + 1) * 512] = (
                 lax.dot_general(kvg[toks, :], w[span, :], RIGHT, preferred_element_type=F32)
                 + lax.dot_general(kvo[...], wo[span, :], RIGHT, preferred_element_type=F32)
             ).astype(BF)
         remote(ph.at[n], h_in.at[n], h_s.at[n], h_r.at[n], peer).start()
-        pltpu.make_async_copy(ph.at[n], ph_out.at[n], out_sem.at[2 + n]).start()
+        pltpu.make_async_copy(ph.at[n], gh.at[2 + n], out_sem.at[2 + n]).start()
         return 0
 
-    lax.fori_loop(0, 4, hidden, 0)
+    lax.fori_loop(0, 2, hidden, 0)
+    for n in range(2):
+        lend(n).wait()
+    borrowed = push(wp, wpo, wo_s.at[1], wo_r.at[1], other)
+
+    def quarter_to(n):
+        return remote(ph.at[2], gh.at[n], h_s.at[2], h_r.at[2], peer)
+
+    keep_quarter = pltpu.make_async_copy(ph.at[2], gh.at[h], out_sem.at[4])
+
+    def quarter():
+        borrowed.wait_recv()
+        for copy in across:
+            copy.wait_recv()
+        for m in range(2):
+            span = part(h * 1024 + m * 512, 512)
+            near = pl.ds(m * 512, 512)
+            value = 0.0
+            for left, right in (
+                (kvg[toks, :], w[span, :]),
+                (kvo[...], wo[span, :]),
+                (kvp[0], wp[near, :]),
+                (kvp[1], wpo[near, :]),
+            ):
+                value = value + lax.dot_general(left, right, RIGHT, preferred_element_type=F32)
+            ph[2, :, m * 512 : (m + 1) * 512] = value.astype(BF)
+        quarter_to(h).start()
+        keep_quarter.start()
+
 
     @pl.when(c == 0)
     def _():
@@ -562,6 +608,8 @@
                 leave(i + AHEAD)
             if i >= LAG:
                 pass_plane(i - LAG, order[i - LAG])
+            if i == 4:
+                quarter()
         for i in range(7):
             remote(zin0.at[i], zin0.at[i], b_s, b_r.at[i], other).wait_recv()
             total[...] += zin0[i].astype(F32)
@@ -580,6 +628,8 @@
                 )
 
         for m in (3, 2, 1, 0):
+            if m == 1:
+                quarter()
             for n, e in enumerate((2, 1, -1, 0)):
                 top = 4 if n < 2 else 3
                 low = 3 if n < 2 else 4
@@ -615,6 +665,9 @@
     keep_own = pltpu.make_async_copy(total.at[rows_of(x, c)], own_out, out_sem.at[6])
     keep_own.start()
     crossing.wait_send()
+    borrowed.wait_send()
+    for copy in across:
+        copy.wait_send()
     all_sent(x_in, bx_s, mate)
     all_sent(x_in, bz_s, down1)
 
@@ -632,9 +685,12 @@
     for copy in finals:
         copy.wait()
     keep_own.wait()
-    for n in range(4):
+    for n in range(2):
         remote(ph.at[n], h_in.at[n], h_s.at[n], h_r.at[n], peer).wait()
-        pltpu.make_async_copy(ph.at[n], ph_out.at[n], out_sem.at[2 + n]).wait()
+        pltpu.make_async_copy(ph.at[n], gh.at[2 + n], out_sem.at[2 + n]).wait()
+    quarter_to(h).wait_send()
+    quarter_to(1 - h).wait_recv()
+    keep_quarter.wait()
 
 
 def run(wk, wv, hid, q, do, seg, table):
@@ -650,19 +706,19 @@
     buffers = [
         pltpu.VMEM((128, 128), jnp.int32), f32(640, 128),
         f32(256, 128), f32(256, 128), f32(16, 1024),
-        bf(2, 32, 256), bf(4096, 256), bf(4096, 256), bf(256, 4096), bf(4096, 256),
+        bf(2, 32, 256), bf(4096, 256), bf(4096, 256), bf(1024, 256), bf(1024, 256), bf(256, 4096), bf(4096, 256),
         bf(128, 512), bf(128, 512), bf(128, 512), bf(128, 512), bf(2, 2560, 128),
         bf(1024, 128), bf(1024, 128), bf(128, 1024), bf(128, 1024), f32(2304, 1024),
         bf(9, 256, 256), bf(2, 128, 512), bf(2, 128, 512),
-        bf(4, 256, 256), bf(5, 256, 256), bf(5, 256, 256), bf(256, 256), bf(128, 256),
-        bf(4096, 256), bf(4, 128, 1024),
+        bf(4, 256, 256), bf(5, 256, 256), bf(5, 256, 256), bf(256, 256), bf(128, 256), bf(2, 128, 256),
+        bf(4096, 256), bf(3, 128, 1024),
         bf(8, 128, 256), bf(8, 2, 128, 256), bf(7, 128, 256), bf(7, 128, 256),
         bf(4, 4, 128, 256), bf(4, 4, 128, 256), bf(3, 128, 256), bf(3, 128, 256),
         f32(128, 256),
     ]
     counts = [
-        0, 3, 0, 32, 0, 0, 5, 5, 0, 0, 0, 16, 0, 4, 0, 16,
-        0, 16, 0, 0, 4, 4, 8, 0, 16, 0, 16, 0, 3, 3, 3, 3, 7, 6,
+        0, 3, 0, 32, 0, 0, 2, 2, 5, 5, 2, 2, 0, 16, 0, 4, 0, 16,
+        0, 16, 3, 3, 3, 3, 8, 0, 16, 0, 16, 0, 3, 3, 3, 3, 7, 6,
     ]
     return pl.pallas_call(
         kernel,
@@ -670,7 +726,7 @@
             shape((128, 1024), BF),
             shape((128, 1024), BF),
             shape((4, 128, 1024), BF),
-            shape((4, 128, 1024), BF),
+            shape((2, 128, 1024), BF),
             shape((32, 256), F32),
             shape((3, 32, 256), F32),
         ),
@@ -686,7 +742,7 @@
 
 def last_kernel(
     att_in, gq_in, ph_in, h_in, own_in, f_in, att, gq, gh, gk, gv,
-    ph, hb, at, qt, own, f, gsum, gkb, gvb, sem_in, sem_out
+    ph, hb, at, qt, own, f, gkb, gvb, sem_in, sem_out
 ):
     def load(src, dst, n):
         copy = pltpu.make_async_copy(src, dst, sem_in.at[n])
@@ -699,7 +755,8 @@
         return copy
 
     parts = [
-        (load(ph_in.at[n], ph.at[n], n), load(h_in.at[n], hb.at[n], 4 + n)) for n in range(4)
+        (load(ph_in.at[n], ph.at[n], n),) + ((load(h_in.at[n - 2], hb.at[n - 2], 4 + n),) if n > 1 else ())
+        for n in range(4)
     ]
     small = [load(own_in, own, 8), load(f_in, f, 9)]
     whole = [load(att_in, at, 10), load(gq_in, qt, 11)]
@@ -707,9 +764,9 @@
     for n in range(4):
         for copy in parts[n]:
             copy.wait()
-        gsum[:, n * 1024 : (n + 1) * 1024] = (ph[n].astype(F32) + hb[n].astype(F32)).astype(BF)
-        cols = pl.ds(n * 1024, 1024)
-        stores.append(store(gsum.at[:, cols], gh.at[:, cols], n))
+        if n > 1:
+            ph[n] = (ph[n].astype(F32) + hb[n - 2].astype(F32)).astype(BF)
+        stores.append(store(ph.at[n], gh.at[:, pl.ds(n * 1024, 1024)], n))
     for n, (copy, src, dst) in enumerate(((whole[0], at, att), (whole[1], qt, gq))):
         copy.wait()
         stores.append(store(src, dst, 4 + n))
@@ -746,12 +803,11 @@
         out_specs=(ANY,) * 5,
         scratch_shapes=[
             pltpu.VMEM((4, 128, 1024), BF),
-            pltpu.VMEM((4, 128, 1024), BF),
+            pltpu.VMEM((2, 128, 1024), BF),
             pltpu.VMEM((128, 1024), BF),
             pltpu.VMEM((128, 1024), BF),
             pltpu.VMEM((32, 256), F32),
             pltpu.VMEM((3, 32, 256), F32),
-            pltpu.VMEM((128, 4096), BF),
             pltpu.VMEM((32, 256), F32),
             pltpu.VMEM((32, 256), F32),
             dma((12,)),

time: 104 us -> 101 us (0.971)
  Pallas kernels: 103 us -> 99.7 us
    pallas_call x1, Pallas kernels: 100 us -> 97.3 us  [run(): pl.pallas_call(kernel, out_shape=(shape((128, 1024), BF), shape((128, 102...]
where the time goes in v7:
time: 101 us; the launch traced here: 100 us
  Pallas kernels  99.7 us (99%)
    pallas_call x1, Pallas kernels, run(): pl.pallas_call(kernel, out_shape=(shape((128, 1024), BF), shape((128, 102...  97.3 us
    pallas_call x1, Pallas kernels, last(): pl.pallas_call(last_kernel, out_shape=results, in_specs=[ANY] * 6, out_sp...  2.47 us

profile of v7, /device:TPU:1, one launch (start us, length us, event | category | flops | bytes accessed | tf_op | source)
XLA Modules:
  0.0 100.4 jit_solution(7858015170111141835)
XLA Ops:
  0.6 97.3 %layer.1 = (bf16[128,1024]{1,0:T(8,128)(2,1)}, bf16[128,1024]{1,0:T(8,128)(2,1)}, bf16[4,128,1024]{2,1,0:T(8,128)(2,1)}, bf16[2,128,1024]{2,1,0:T(8,128)(2,1)}, ...) custom-call(bf16[32,256]{1,0:T(8,128)(2,1)} %wk.1, bf16[32,256]{1,0:T(8,128)(2,1)} %wv.1, bf16[128,4096]{1,0:T(8,128)(2,1)} %hid.1, ...), custom_call_target="tpu_custom_call" | custom-call | tf_op jit(solution)/shard_map/layer/pallas_call | solution.py:723
  97.9 2.5 %last.1 = (bf16[128,1024]{1,0:T(8,128)(2,1)}, bf16[128,1024]{1,0:T(8,128)(2,1)}, bf16[128,4096]{1,0:T(8,128)(2,1)}, f32[32,256]{1,0:T(8,128)}, f32[32,256]{1,0:T(8,128)}) custom-call(bf16[128,1024]{1,0:T(8,128)(2,1)} %get-tuple-element.11.att_in, bf16[128,1024]{1,0:T(8,128)(2,1)} %get-tuple-element.12.gq_in, bf16[4,128,1024]{2,1,0:T(8,128)(2,1)} %get-tuple-element.13.ph_in, ...), custom_call_target="tpu_custom_call" | custom-call | tf_op jit(solution)/shard_map/last/pallas_call | solution.py:799

commit v8 on v7

--- a/solution.py
+++ b/solution.py
@@ -234,7 +234,6 @@
             q_s.at[n], q_r.at[n], peer,
         )
 
-    lend(0).start()
 
     def project(n, sums):
         span = part(n * 1024, 1024)
@@ -269,6 +268,8 @@
     def _():
         for n in range(4):
             window_across(4, n).start()
+
+    lend(0).start()
 
     for t in range(2):
         @pl.when(c == t)

time: 101 us -> 103 us (1.020)
  Pallas kernels: 99.7 us -> 102 us
    pallas_call x1, Pallas kernels: 97.3 us -> 99.4 us  [run(): pl.pallas_call(kernel, out_shape=(shape((128, 1024), BF), shape((128, 102...]
where the time goes in v8:
time: 103 us; the launch traced here: 102 us
  Pallas kernels  102 us (99%)
    pallas_call x1, Pallas kernels, run(): pl.pallas_call(kernel, out_shape=(shape((128, 1024), BF), shape((128, 102...  99.4 us
    pallas_call x1, Pallas kernels, last(): pl.pallas_call(last_kernel, out_shape=results, in_specs=[ANY] * 6, out_sp...  2.47 us

profile of v8, /device:TPU:1, one launch (start us, length us, event | category | flops | bytes accessed | tf_op | source)
XLA Modules:
  0.0 102.5 jit_solution(17702748490802284972)
XLA Ops:
  0.6 99.4 %layer.1 = (bf16[128,1024]{1,0:T(8,128)(2,1)}, bf16[128,1024]{1,0:T(8,128)(2,1)}, bf16[4,128,1024]{2,1,0:T(8,128)(2,1)}, bf16[2,128,1024]{2,1,0:T(8,128)(2,1)}, ...) custom-call(bf16[32,256]{1,0:T(8,128)(2,1)} %wk.1, bf16[32,256]{1,0:T(8,128)(2,1)} %wv.1, bf16[128,4096]{1,0:T(8,128)(2,1)} %hid.1, ...), custom_call_target="tpu_custom_call" | custom-call | tf_op jit(solution)/shard_map/layer/pallas_call | solution.py:724
  100.0 2.5 %last.1 = (bf16[128,1024]{1,0:T(8,128)(2,1)}, bf16[128,1024]{1,0:T(8,128)(2,1)}, bf16[128,4096]{1,0:T(8,128)(2,1)}, f32[32,256]{1,0:T(8,128)}, f32[32,256]{1,0:T(8,128)}) custom-call(bf16[128,1024]{1,0:T(8,128)(2,1)} %get-tuple-element.11.att_in, bf16[128,1024]{1,0:T(8,128)(2,1)} %get-tuple-element.12.gq_in, bf16[4,128,1024]{2,1,0:T(8,128)(2,1)} %get-tuple-element.13.ph_in, ...), custom_call_target="tpu_custom_call" | custom-call | tf_op jit(solution)/shard_map/last/pallas_call | solution.py:800
